TPU v7x, 256 devices: a whole 4x4x8 slice. The times are simulated.
256 devices in a mesh: row: 32 (over x, z), col: 8 (over y, core).
Axes of the slice: x: 4, y: 4, z: 8, core: 2. Of those that a mesh axis runs over, the one named last changes fastest.
Arguments:
- a_blocks: bfloat16 [32, 8, 64, 65536], P('row', 'col'), may hold values from -0.75 to 0.75
- a_rows: int32 [32, 8, 1024], P('row', 'col'), may hold values from 0 to 255
- a_steps: int32 [32, 8, 1024], P('row', 'col'), may hold values from 0 to 2
- a_cols: int32 [32, 8, 1024], P('row', 'col'), may hold values from 0 to 65
- a_live: int32 [32, 8], P('row', 'col'), may hold values from 256 to 1024, as said below
- p_blocks: bfloat16 [128, 512, 64, 128], P('row', 'col'), may hold values from -0.8984375 to 0.8984375
Outputs:
- coarse_op: float32 [4096, 9216], P('row', 'col')
Inputs may be any that keep to these rules, and one draw needn't show every extreme that they name: `a_live`: blocks at or beyond a device's count are padding; one device in every draw holds 1024 live blocks.
All inputs are finite; a program needn't handle non-finite values.
Results may differ from a plain program's by a relative error of at most 0.0029.
Values may be sent and summed in bfloat16 or wider, within the bound.
No kernel may reach another device: no remote copies, remote signals or barrier semaphores. Data moves between devices by JAX's collectives and lax.ppermute only.
A program may use at most 192 MiB of HBM per device.

v0:
```python
import jax
import jax.numpy as jnp
from jax import lax
from jax.sharding import PartitionSpec as P

AGG_DEV = 2


def extended_2(x, sides, width):
    for axis, dim in sides:
        peers, length = (lax.axis_size(axis), x.shape[dim])
        up = [(i, (i + 1) % peers) for i in range(peers - 1)]
        down = [(j, i) for i, j in up]
        last = lax.slice_in_dim(x, length - width, length, axis=dim)
        leading = lax.slice_in_dim(x, 0, width, axis=dim)
        before = lax.ppermute(last, axis, up)
        after = lax.ppermute(leading, axis, down)
        x = jnp.concatenate([before, x, after], axis=dim)
    return x


def shifted(value, axis, steps):
    count = lax.axis_size(axis)
    leading, last = (max(0, -steps), min(count, count - steps))
    return lax.ppermute(value, axis, [(source, source + steps) for source in range(leading, last)])


def slot_targets(cell_x, cell_y, row_dev, span_x, span_y, aggr_count, row_count):
    owner_x = (cell_x + span_x) // span_x - 1
    owner_y = (cell_y + span_y) // span_y - 1
    local_u = cell_x - owner_x * span_x
    local_v = cell_y - owner_y * span_y
    band_id = local_v // (span_y // aggr_count)
    owner_row = row_dev + owner_x
    step_up = jnp.logical_and(local_u == span_x - 1, owner_row < row_count - 1).astype(jnp.int32)
    step_down = jnp.logical_and(local_u == 0, owner_row > 0).astype(jnp.int32)
    shift_x = step_up - step_down
    second_band = jnp.where(shift_x != 0, band_id, (band_id + 1) % aggr_count)
    offset_x = jnp.stack([owner_x, owner_x + shift_x], axis=-1)
    offset_y = jnp.stack([owner_y, owner_y], axis=-1)
    band_ids = jnp.stack([band_id, second_band], axis=-1)
    return (offset_x, offset_y, band_ids)


def block_layout(row_ids, step_ids, col_ids, row_dev, span_x, span_y, aggr_count, row_count):
    row_x = row_ids // span_y
    row_y = row_ids % span_y
    col_x = row_x + step_ids - 1
    outside = jnp.logical_or(col_x < 0, col_x >= span_x)
    col_y = jnp.where(outside, jnp.clip(col_ids - 1, 0, span_y - 1), col_ids - 1)
    ext_width = span_y + 2
    row_cell = (row_x + 1) * ext_width + row_y + 1
    col_cell = (col_x + 1) * ext_width + col_y + 1
    left_side = slot_targets(row_x, row_y, row_dev, span_x, span_y, aggr_count, row_count)
    right_side = slot_targets(col_x, col_y, row_dev, span_x, span_y, aggr_count, row_count)
    amount = row_ids.shape[0]
    group_ids = (
        (right_side[0][:, None, :] - left_side[0][:, :, None] + 1) * 3
        + right_side[1][:, None, :]
        + 1
    )
    slot_part = jnp.broadcast_to(left_side[0][:, :, None] + 1, (amount, 2, 2))
    slot_row = jnp.broadcast_to(left_side[2][:, :, None], (amount, 2, 2))
    slot_col = group_ids * aggr_count + right_side[2][:, None, :]
    return (row_cell, col_cell, slot_part, slot_row, slot_col)


def on_device(a_blocks, a_rows, a_steps, a_cols, a_live, p_blocks):
    block_size = a_blocks.shape[2]
    capacity = a_rows.shape[2]
    span_x = p_blocks.shape[0]
    span_y = p_blocks.shape[1]
    slot_width = p_blocks.shape[3]
    slot_count = slot_width // block_size
    aggr_count = AGG_DEV
    row_count = lax.axis_size("row")
    row_dev = lax.axis_index("row")
    row_kinds = 3 * aggr_count
    col_kinds = 9 * aggr_count
    extended = extended_2(p_blocks, (("row", 0), ("col", 1)), 1)
    rows_table = extended.reshape((span_x + 2) * (span_y + 2), block_size, slot_width)
    matrix = a_blocks.reshape(block_size, capacity, block_size)
    live_count = a_live.reshape(())
    row_cell, col_cell, slot_part, slot_row, slot_col = block_layout(
        a_rows.reshape(capacity),
        a_steps.reshape(capacity),
        a_cols.reshape(capacity),
        row_dev,
        span_x,
        span_y,
        aggr_count,
        row_count,
    )
    row_target = slot_part * aggr_count + slot_row
    group_size = min(256, capacity)
    row_range = jnp.arange(row_kinds, dtype=jnp.int32)
    col_range = jnp.arange(col_kinds, dtype=jnp.int32)

    def add_group(loop_step, partial_value):
        first_block = loop_step * group_size
        a_piece = lax.dynamic_slice_in_dim(matrix, first_block, group_size, 1)
        left_rows = rows_table[lax.dynamic_slice_in_dim(row_cell, first_block, group_size, 0)]
        right_rows = rows_table[lax.dynamic_slice_in_dim(col_cell, first_block, group_size, 0)]
        product = jnp.einsum(
            "xnb,nbk->nxk", a_piece, right_rows, preferred_element_type=jnp.float32
        ).astype(jnp.bfloat16)
        contribs = jnp.einsum(
            "nxa,nxb->nab", left_rows, product, preferred_element_type=jnp.float32
        )
        contribs = contribs.reshape(group_size, slot_count, block_size, slot_count, block_size)
        keep_mask = (first_block + jnp.arange(group_size, dtype=jnp.int32) < live_count).astype(
            jnp.float32
        )
        row_here = lax.dynamic_slice_in_dim(row_target, first_block, group_size, 0)
        col_here = lax.dynamic_slice_in_dim(slot_col, first_block, group_size, 0)
        row_hot = (row_here[:, :, :, None] == row_range).astype(jnp.float32)
        col_hot = (col_here[:, :, :, None] == col_range).astype(jnp.float32)
        placing = (
            row_hot[:, :, :, :, None]
            * col_hot[:, :, :, None, :]
            * keep_mask[:, None, None, None, None]
        )
        return partial_value + jnp.einsum(
            "nstrc,nsmtk->rmck", placing, contribs, precision=lax.Precision.HIGHEST
        )

    empty_sum = jnp.zeros((row_kinds, block_size, col_kinds, block_size), jnp.float32)
    partial_value = lax.fori_loop(0, capacity // group_size, add_group, empty_sum)
    partial_value = partial_value.reshape(3, aggr_count * block_size, col_kinds * block_size)
    own_rows = partial_value[1]
    from_below = shifted(partial_value[2], "row", 1)
    from_above = shifted(partial_value[0], "row", -1)
    summed = own_rows + from_below + from_above
    return summed


def solution(mesh):
    return jax.shard_map(
        on_device,
        mesh=mesh,
        in_specs=(
            P("row", "col", None, None),
            P("row", "col", None),
            P("row", "col", None),
            P("row", "col", None),
            P("row", "col"),
            P("row", "col", None, None),
        ),
        out_specs=P("row", "col"),
        check_vma=False,
    )
```

profile of v0, /device:TPU:16, one launch (start us, length us, event | category | flops | bytes accessed | tf_op | source)
XLA Modules:
  0.0 431.0 jit_solution(16477762141330480762)
XLA Ops:
  10.3 18.9 %collective-permute-done = bf16[1,64,64,128]{3,2,1,0:T(8,128)(2,1)S(1)} collective-permute-done((bf16[1,64,64,128]{3,2,1,0:T(8,128)(2,1)}, bf16[1,64,64,128]{3,2,1,0:T(8,128)(2,1)S(1)}, u32[]{:S(2)}, u32[]{:S(2)}) %collective-permute-start) | collective-permute-done | bytes 1048608 | tf_op jit(solution)/shard_map/ppermute | solution.py:16
  41.7 18.1 %reshape.813 = bf16[64,1024,64]{2,1,0:T(8,128)(2,1)} reshape(bf16[1,1,64,65536]{3,2,1,0:T(8,128)(2,1)} %param.8) | data formatting | bytes 16777216 | tf_op jit(solution)/shard_map/reshape | solution.py:82
  59.8 6.7 %pad_maximum_fusion = bf16[6,66,64,128]{3,2,1,0:T(8,128)(2,1)} fusion(bf16[6,1,64,128]{3,2,1,0:T(8,128)(2,1)S(1)} %collective-permute-done.3, bf16[6,64,64,128]{3,2,1,0:T(8,128)(2,1)} %copy-done, bf16[6,1,64,128]{3,2,1,0:T(8,128)(2,1)S(1)} %collective-permute-done.2), kind=kLoop, calls=%fused_computation.23 | loop fusion | flops 6488064 | bytes 12976128 | tf_op jit(solution)/shard_map/concatenate | solution.py:18
  66.5 326.1 %while.14 = (s32[]{:T(128)}, f32[6,64,18,64]{3,2,0,1:T(8,128)}, s32[1024]{0:T(1024)S(1)}, bf16[396,64,128]{2,1,0:T(8,128)(2,1)}, bf16[64,1024,64]{2,1,0:T(8,128)...) while((s32[]{:T(128)}, f32[6,64,18,64]{3,2,0,1:T(8,128)}, ...), condition=%wide.region_1.2_spmd.clone, body=%wide.region_0.1_spmd.clone.sunk | while | flops 6244380672 | bytes 105883848 | solution.py:128
  66.8 6.0 %gather_fusion = bf16[256,64,128]{2,1,0:T(8,128)(2,1)} fusion(bf16[396,64,128]{2,1,0:T(8,128)(2,1)} %get-tuple-element.365, s32[1024]{0:T(1024)S(1)} %pad_clamp_fusion.4), kind=kCustom, calls=%fused_computation.clone.clone.1 | custom fusion | bytes 8389632 | tf_op jit(solution)/shard_map/while/body/eval_jaxpr/gather | solution.py:102
  72.8 5.9 %gather_fusion.1 = bf16[256,64,128]{2,1,0:T(8,128)(2,1)} fusion(bf16[396,64,128]{2,1,0:T(8,128)(2,1)} %get-tuple-element.365, s32[1024]{0:T(1024)S(1)} %pad_clamp_fusion.5), kind=kCustom, calls=%fused_computation.1.clone.clone.1 | custom fusion | bytes 8389632 | tf_op jit(solution)/shard_map/while/body/eval_jaxpr/gather | solution.py:103
  78.8 4.6 %constant_dynamic-slice_fusion.5 = bf16[64,256,64]{2,1,0:T(8,128)(2,1)} fusion(bf16[64,1024,64]{2,1,0:T(8,128)(2,1)} %get-tuple-element.366, s32[]{:T(128)S(6)} %select_n.327), kind=kLoop, calls=%fused_computation.22.clone.1 | loop fusion | bytes 4194308 | tf_op jit(solution)/shard_map/while/body/eval_jaxpr/dynamic_slice | solution.py:101
  83.4 12.8 %fusion.56 = f32[256,128,128]{2,1,0:T(8,128)} fusion(bf16[256,64,128]{2,1,0:T(8,128)(2,1)} %gather_fusion, bf16[256,64,128]{2,1,0:T(8,128)(2,1)} %gather_fusion.1, bf16[64,256,64]{2,1,0:T(8,128)(2,1)} %constant_dynamic-slice_fusion.5), kind=kOutput, calls=%fused_computation.7.clone.1 | convolution fusion | flops 807403520 | bytes 27262976 | tf_op jit(solution)/shard_map/while/body/eval_jaxpr/nxa,nxb->nab/dot_general | solution.py:107
  96.2 17.8 %copy.39 = f32[256,128,128]{0,2,1:T(8,128)} copy(f32[256,128,128]{2,1,0:T(8,128)} %fusion.56) | data formatting | bytes 33554432 | tf_op jit(solution)/shard_map/while/body/eval_jaxpr/nxa,nxb->nab/dot_general | solution.py:107
  114.6 27.6 %fusion.58 = f32[64,64,6,18,1,1]{1,3,5,0,2,4:T(8,128)} fusion(f32[256,2,64,2,64,1]{0,4,3,2,5,1:T(8,128)} %bitcast.66, f32[256]{0:T(256)S(1)} %compare_convert_fusion.4, f32[256,2,2,18]{0,3,2,1:T(8,128)S(1)} %fusion.57, f32[256,2,2,6]{0,2,1,3:T(2,128)S(1)} %compare_convert_fusion.5), kind=kOutput, calls=%fused_computation.9.clone.1 | convolution fusion | flops 5436039168 | bytes 18646016 | tf_op jit(solution)/shard_map/while/body/eval_jaxpr/nstrc,nsmtk->rmck/dot_general | solution.py:123
  142.2 4.9 %bitcast_add_fusion.3 = f32[6,64,18,64]{3,2,0,1:T(8,128)} fusion(f32[64,64,6,18,1,1]{1,3,5,0,2,4:T(8,128)} %fusion.58, f32[6,64,18,64]{3,2,0,1:T(8,128)} %get-tuple-element.350, pred[]{:T(512)S(6)} %compare.182), kind=kLoop, calls=%fused_computation.4.clone.1 | loop fusion | flops 884736 | bytes 5308417 | tf_op jit(solution)/shard_map/while/body/eval_jaxpr/add | solution.py:123
  147.2 6.0 %gather_fusion = bf16[256,64,128]{2,1,0:T(8,128)(2,1)} fusion(bf16[396,64,128]{2,1,0:T(8,128)(2,1)} %get-tuple-element.365, s32[1024]{0:T(1024)S(1)} %pad_clamp_fusion.4), kind=kCustom, calls=%fused_computation.clone.clone.1 | custom fusion | bytes 8389632 | tf_op jit(solution)/shard_map/while/body/eval_jaxpr/gather | solution.py:102
  153.2 5.9 %gather_fusion.1 = bf16[256,64,128]{2,1,0:T(8,128)(2,1)} fusion(bf16[396,64,128]{2,1,0:T(8,128)(2,1)} %get-tuple-element.365, s32[1024]{0:T(1024)S(1)} %pad_clamp_fusion.5), kind=kCustom, calls=%fused_computation.1.clone.clone.1 | custom fusion | bytes 8389632 | tf_op jit(solution)/shard_map/while/body/eval_jaxpr/gather | solution.py:103
  159.1 4.6 %constant_dynamic-slice_fusion.5 = bf16[64,256,64]{2,1,0:T(8,128)(2,1)} fusion(bf16[64,1024,64]{2,1,0:T(8,128)(2,1)} %get-tuple-element.366, s32[]{:T(128)S(6)} %select_n.327), kind=kLoop, calls=%fused_computation.22.clone.1 | loop fusion | bytes 4194308 | tf_op jit(solution)/shard_map/while/body/eval_jaxpr/dynamic_slice | solution.py:101
  163.8 12.8 %fusion.56 = f32[256,128,128]{2,1,0:T(8,128)} fusion(bf16[256,64,128]{2,1,0:T(8,128)(2,1)} %gather_fusion, bf16[256,64,128]{2,1,0:T(8,128)(2,1)} %gather_fusion.1, bf16[64,256,64]{2,1,0:T(8,128)(2,1)} %constant_dynamic-slice_fusion.5), kind=kOutput, calls=%fused_computation.7.clone.1 | convolution fusion | flops 807403520 | bytes 27262976 | tf_op jit(solution)/shard_map/while/body/eval_jaxpr/nxa,nxb->nab/dot_general | solution.py:107
  176.6 17.8 %copy.39 = f32[256,128,128]{0,2,1:T(8,128)} copy(f32[256,128,128]{2,1,0:T(8,128)} %fusion.56) | data formatting | bytes 33554432 | tf_op jit(solution)/shard_map/while/body/eval_jaxpr/nxa,nxb->nab/dot_general | solution.py:107
  195.0 27.6 %fusion.58 = f32[64,64,6,18,1,1]{1,3,5,0,2,4:T(8,128)} fusion(f32[256,2,64,2,64,1]{0,4,3,2,5,1:T(8,128)} %bitcast.66, f32[256]{0:T(256)S(1)} %compare_convert_fusion.4, f32[256,2,2,18]{0,3,2,1:T(8,128)S(1)} %fusion.57, f32[256,2,2,6]{0,2,1,3:T(2,128)S(1)} %compare_convert_fusion.5), kind=kOutput, calls=%fused_computation.9.clone.1 | convolution fusion | flops 5436039168 | bytes 18646016 | tf_op jit(solution)/shard_map/while/body/eval_jaxpr/nstrc,nsmtk->rmck/dot_general | solution.py:123
  222.6 6.4 %bitcast_add_fusion.3 = f32[6,64,18,64]{3,2,0,1:T(8,128)} fusion(f32[64,64,6,18,1,1]{1,3,5,0,2,4:T(8,128)} %fusion.58, f32[6,64,18,64]{3,2,0,1:T(8,128)} %get-tuple-element.350, pred[]{:T(512)S(6)} %compare.182), kind=kLoop, calls=%fused_computation.4.clone.1 | loop fusion | flops 884736 | bytes 5308417 | tf_op jit(solution)/shard_map/while/body/eval_jaxpr/add | solution.py:123
  229.1 6.0 %gather_fusion = bf16[256,64,128]{2,1,0:T(8,128)(2,1)} fusion(bf16[396,64,128]{2,1,0:T(8,128)(2,1)} %get-tuple-element.365, s32[1024]{0:T(1024)S(1)} %pad_clamp_fusion.4), kind=kCustom, calls=%fused_computation.clone.clone.1 | custom fusion | bytes 8389632 | tf_op jit(solution)/shard_map/while/body/eval_jaxpr/gather | solution.py:102
  235.1 5.9 %gather_fusion.1 = bf16[256,64,128]{2,1,0:T(8,128)(2,1)} fusion(bf16[396,64,128]{2,1,0:T(8,128)(2,1)} %get-tuple-element.365, s32[1024]{0:T(1024)S(1)} %pad_clamp_fusion.5), kind=kCustom, calls=%fused_computation.1.clone.clone.1 | custom fusion | bytes 8389632 | tf_op jit(solution)/shard_map/while/body/eval_jaxpr/gather | solution.py:103
  245.6 12.8 %fusion.56 = f32[256,128,128]{2,1,0:T(8,128)} fusion(bf16[256,64,128]{2,1,0:T(8,128)(2,1)} %gather_fusion, bf16[256,64,128]{2,1,0:T(8,128)(2,1)} %gather_fusion.1, bf16[64,256,64]{2,1,0:T(8,128)(2,1)} %constant_dynamic-slice_fusion.5), kind=kOutput, calls=%fused_computation.7.clone.1 | convolution fusion | flops 807403520 | bytes 27262976 | tf_op jit(solution)/shard_map/while/body/eval_jaxpr/nxa,nxb->nab/dot_general | solution.py:107
  258.4 17.8 %copy.39 = f32[256,128,128]{0,2,1:T(8,128)} copy(f32[256,128,128]{2,1,0:T(8,128)} %fusion.56) | data formatting | bytes 33554432 | tf_op jit(solution)/shard_map/while/body/eval_jaxpr/nxa,nxb->nab/dot_general | solution.py:107
  276.9 27.6 %fusion.58 = f32[64,64,6,18,1,1]{1,3,5,0,2,4:T(8,128)} fusion(f32[256,2,64,2,64,1]{0,4,3,2,5,1:T(8,128)} %bitcast.66, f32[256]{0:T(256)S(1)} %compare_convert_fusion.4, f32[256,2,2,18]{0,3,2,1:T(8,128)S(1)} %fusion.57, f32[256,2,2,6]{0,2,1,3:T(2,128)S(1)} %compare_convert_fusion.5), kind=kOutput, calls=%fused_computation.9.clone.1 | convolution fusion | flops 5436039168 | bytes 18646016 | tf_op jit(solution)/shard_map/while/body/eval_jaxpr/nstrc,nsmtk->rmck/dot_general | solution.py:123
  304.4 6.4 %bitcast_add_fusion.3 = f32[6,64,18,64]{3,2,0,1:T(8,128)} fusion(f32[64,64,6,18,1,1]{1,3,5,0,2,4:T(8,128)} %fusion.58, f32[6,64,18,64]{3,2,0,1:T(8,128)} %get-tuple-element.350, pred[]{:T(512)S(6)} %compare.182), kind=kLoop, calls=%fused_computation.4.clone.1 | loop fusion | flops 884736 | bytes 5308417 | tf_op jit(solution)/shard_map/while/body/eval_jaxpr/add | solution.py:123
  310.9 6.0 %gather_fusion = bf16[256,64,128]{2,1,0:T(8,128)(2,1)} fusion(bf16[396,64,128]{2,1,0:T(8,128)(2,1)} %get-tuple-element.365, s32[1024]{0:T(1024)S(1)} %pad_clamp_fusion.4), kind=kCustom, calls=%fused_computation.clone.clone.1 | custom fusion | bytes 8389632 | tf_op jit(solution)/shard_map/while/body/eval_jaxpr/gather | solution.py:102
  316.9 5.9 %gather_fusion.1 = bf16[256,64,128]{2,1,0:T(8,128)(2,1)} fusion(bf16[396,64,128]{2,1,0:T(8,128)(2,1)} %get-tuple-element.365, s32[1024]{0:T(1024)S(1)} %pad_clamp_fusion.5), kind=kCustom, calls=%fused_computation.1.clone.clone.1 | custom fusion | bytes 8389632 | tf_op jit(solution)/shard_map/while/body/eval_jaxpr/gather | solution.py:103
  327.4 12.8 %fusion.56 = f32[256,128,128]{2,1,0:T(8,128)} fusion(bf16[256,64,128]{2,1,0:T(8,128)(2,1)} %gather_fusion, bf16[256,64,128]{2,1,0:T(8,128)(2,1)} %gather_fusion.1, bf16[64,256,64]{2,1,0:T(8,128)(2,1)} %constant_dynamic-slice_fusion.5), kind=kOutput, calls=%fused_computation.7.clone.1 | convolution fusion | flops 807403520 | bytes 27262976 | tf_op jit(solution)/shard_map/while/body/eval_jaxpr/nxa,nxb->nab/dot_general | solution.py:107
  340.2 17.8 %copy.39 = f32[256,128,128]{0,2,1:T(8,128)} copy(f32[256,128,128]{2,1,0:T(8,128)} %fusion.56) | data formatting | bytes 33554432 | tf_op jit(solution)/shard_map/while/body/eval_jaxpr/nxa,nxb->nab/dot_general | solution.py:107
  358.7 27.6 %fusion.58 = f32[64,64,6,18,1,1]{1,3,5,0,2,4:T(8,128)} fusion(f32[256,2,64,2,64,1]{0,4,3,2,5,1:T(8,128)} %bitcast.66, f32[256]{0:T(256)S(1)} %compare_convert_fusion.4, f32[256,2,2,18]{0,3,2,1:T(8,128)S(1)} %fusion.57, f32[256,2,2,6]{0,2,1,3:T(2,128)S(1)} %compare_convert_fusion.5), kind=kOutput, calls=%fused_computation.9.clone.1 | convolution fusion | flops 5436039168 | bytes 18646016 | tf_op jit(solution)/shard_map/while/body/eval_jaxpr/nstrc,nsmtk->rmck/dot_general | solution.py:123
  386.3 6.4 %bitcast_add_fusion.3 = f32[6,64,18,64]{3,2,0,1:T(8,128)} fusion(f32[64,64,6,18,1,1]{1,3,5,0,2,4:T(8,128)} %fusion.58, f32[6,64,18,64]{3,2,0,1:T(8,128)} %get-tuple-element.350, pred[]{:T(512)S(6)} %compare.182), kind=kLoop, calls=%fused_computation.4.clone.1 | loop fusion | flops 884736 | bytes 5308417 | tf_op jit(solution)/shard_map/while/body/eval_jaxpr/add | solution.py:123
  402.9 4.7 %collective-permute-start.4 = (f32[128,1152]{0,1:T(8,128)}, f32[128,1152]{0,1:T(8,128)}, u32[]{:S(2)}, u32[]{:S(2)}) collective-permute-start(f32[128,1152]{0,1:T(8,128)} %squeeze.10), channel_id=1, source_target_pairs={{0,8},{8,16},{16,24},{24,32},{32,40},{40,48},{48,56},{56,64},{64,7... | collective-permute-start | bytes 1769480 | tf_op jit(solution)/shard_map/ppermute | solution.py:25
  419.4 9.2 %collective-permute-done.5 = f32[128,1152]{0,1:T(8,128)} collective-permute-done((f32[128,1152]{0,1:T(8,128)S(1)}, f32[128,1152]{0,1:T(8,128)}, u32[]{:S(2)}, u32[]{:S(2)}) %collective-permute-start.5) | collective-permute-done | bytes 589856 | tf_op jit(solution)/shard_map/ppermute | solution.py:25
  (71 shorter events, 59.4 us)
Async XLA Ops:
  2.7 26.5 %collective-permute-start = (bf16[1,64,64,128]{3,2,1,0:T(8,128)(2,1)}, bf16[1,64,64,128]{3,2,1,0:T(8,128)(2,1)S(1)}, u32[]{:S(2)}, u32[]{:S(2)}) collective-permute-start(bf16[1,64,64,128]{3,2,1,0:T(8,128)(2,1)} %get-tuple-element.265), channel_id=1, source_target_pairs={{0,8},{8,16},{16,24},{24,32},{32,40},{40,48},{48,56},{56,64},{64,7... | collective-permute-start | bytes 3145736 | tf_op jit(solution)/shard_map/ppermute | solution.py:16
  6.6 26.6 %collective-permute-start.1 = (bf16[1,64,64,128]{3,2,1,0:T(8,128)(2,1)S(1)}, bf16[1,64,64,128]{3,2,1,0:T(8,128)(2,1)S(1)}, u32[]{:S(2)}, u32[]{:S(2)}) collective-permute-start(bf16[1,64,64,128]{3,2,1,0:T(8,128)(2,1)S(1)} %get-tuple-element.264), channel_id=1, source_target_pairs={{8,0},{16,8},{24,16},{32,24},{40,32},{48,40},{56,48},{64,56},{72,6... | collective-permute-start | bytes 3145736 | tf_op jit(solution)/shard_map/ppermute | solution.py:17
  29.3 12.3 %copy-start.1 = (s32[1,1,1024]{2,1,0:T(1,128)S(1)}, s32[1,1,1024]{2,1,0:T(1,128)}, u32[]{:S(2)}) copy-start(s32[1,1,1024]{2,1,0:T(1,128)} %param.10) | copy-start | bytes 12292
  29.3 12.3 %copy-start.2 = (s32[1,1,1024]{2,1,0:T(1,128)S(1)}, s32[1,1,1024]{2,1,0:T(1,128)}, u32[]{:S(2)}) copy-start(s32[1,1,1024]{2,1,0:T(1,128)} %param.9) | copy-start | bytes 12292
  33.3 2.7 copy-start
  36.0 23.8 %collective-permute-start.2 = (bf16[6,1,64,128]{3,2,1,0:T(8,128)(2,1)S(1)}, bf16[6,1,64,128]{3,2,1,0:T(8,128)(2,1)S(1)}, u32[]{:S(2)}, u32[]{:S(2)}) collective-permute-start(bf16[6,1,64,128]{3,2,1,0:T(8,128)(2,1)S(1)} %get-tuple-element.259), channel_id=1, source_target_pairs={{0,1},{1,2},{2,3},{3,4},{4,5},{5,6},{6,7},{8,9},{9,10},{10,11},{11... | collective-permute-start | bytes 294920 | tf_op jit(solution)/shard_map/ppermute | solution.py:16
  38.0 21.9 %collective-permute-start.3 = (bf16[6,1,64,128]{3,2,1,0:T(8,128)(2,1)S(1)}, bf16[6,1,64,128]{3,2,1,0:T(8,128)(2,1)S(1)}, u32[]{:S(2)}, u32[]{:S(2)}) collective-permute-start(bf16[6,1,64,128]{3,2,1,0:T(8,128)(2,1)S(1)} %get-tuple-element.260), channel_id=1, source_target_pairs={{1,0},{2,1},{3,2},{4,3},{5,4},{6,5},{7,6},{9,8},{10,9},{11,10},{12... | collective-permute-start | bytes 294920 | tf_op jit(solution)/shard_map/ppermute | solution.py:17
  402.9 16.6 %collective-permute-start.4 = (f32[128,1152]{0,1:T(8,128)}, f32[128,1152]{0,1:T(8,128)}, u32[]{:S(2)}, u32[]{:S(2)}) collective-permute-start(f32[128,1152]{0,1:T(8,128)} %squeeze.10), channel_id=1, source_target_pairs={{0,8},{8,16},{16,24},{24,32},{32,40},{40,48},{48,56},{56,64},{64,7... | collective-permute-start | bytes 1769480 | tf_op jit(solution)/shard_map/ppermute | solution.py:25
  411.5 17.2 %collective-permute-start.5 = (f32[128,1152]{0,1:T(8,128)S(1)}, f32[128,1152]{0,1:T(8,128)}, u32[]{:S(2)}, u32[]{:S(2)}) collective-permute-start(f32[128,1152]{0,1:T(8,128)S(1)} %squeeze.11), channel_id=1, source_target_pairs={{8,0},{16,8},{24,16},{32,24},{40,32},{48,40},{56,48},{64,56},{72,6... | collective-permute-start | bytes 1769480 | tf_op jit(solution)/shard_map/ppermute | solution.py:25
where the time goes:
time: 436 us; the launch traced here: 431 us
  local copies, waits for them, and re-layouts  182 us (42%)
  matrix products  161 us (37%)
  other arithmetic  37.6 us (9%)
  waiting for transfers between devices  33.1 us (8%)
  starting transfers between devices  16.7 us (4%)
    dot_general x4, matrix products, add_group(): jnp.einsum('nstrc,nsmtk->rmck', placing, contribs, precision=lax.Precisio...  110 us
    dot_general x4, local copies, waits for them, and re-layouts, add_group(): jnp.einsum('nxa,nxb->nab', left_rows, product, preferred_element_type=jnp...  71.1 us
    dot_general x4, matrix products, add_group(): jnp.einsum('nxa,nxb->nab', left_rows, product, preferred_element_type=jnp...  51.2 us
    gather x4, local copies, waits for them, and re-layouts, add_group(): rows_table[lax.dynamic_slice_in_dim(row_cell, first_block, group_size, 0)]  24 us
    add x4, other arithmetic, add_group(): partial_value + jnp.einsum('nstrc,nsmtk->rmck', placing, contribs, precis...  24 us
    gather x4, local copies, waits for them, and re-layouts, add_group(): rows_table[lax.dynamic_slice_in_dim(col_cell, first_block, group_size, 0)]  23.6 us
    ppermute x2, waiting for transfers between devices, extended_2(): before = lax.ppermute(last, axis, up)  18.9 us
    dynamic_slice x4, local copies, waits for them, and re-layouts, add_group(): a_piece = lax.dynamic_slice_in_dim(matrix, first_block, group_size, 1)  18.5 us
  transfers between devices with their start and end apart: 6, of which 4 were waited for; matrix products, arithmetic and copies ran while one was open for 7% of the time, Pallas kernels for 0%

commit v1 on v0

v1 whole, which is shorter than its diff:
```python
import functools

import jax
import jax.numpy as jnp
from jax import lax
from jax.experimental import pallas as pl
from jax.experimental.pallas import tpu as pltpu
from jax.sharding import PartitionSpec as P

B = 64
W2 = 128
SX, SY = 4, 64
FINE = SX * SY
HALF = SY // 2
TRASH_Z = 3 * FINE
N_WX = 128
N_W = N_WX + 32
TRASH_W = N_W
GROUP = 64
DEPTH = 4
FAR = 32
PT_STEPS = 1
UP_AT, DN_AT, SUMS = 3 * W2, 5 * W2, 7 * W2
SPARE_SUMS, SPARE_W = 144, 32
TAIL_VMEM = 24
MIB = 1024 * 1024
CHUNK = 128
f32, bf16 = jnp.float32, jnp.bfloat16


def swap_slots(x):
    return jnp.concatenate([x[..., B:], x[..., :B]], axis=-1)


def lanes_low(rows):
    return lax.broadcasted_iota(jnp.int32, (rows, W2), 1) < B


def roll(x):
    return pltpu.roll(x, B, 1)


def add_two(ref, i, j, x, y):
    old_i, old_j = ref[i], ref[j]
    new_i = old_i + x
    ref[i] = new_i
    ref[j] = jnp.where(i == j, new_i, old_j) + y


def main_kernel(scal, ci_ref, zi_ref, hp_ref, a_hbm, p_hbm,
                sums_hbm, wt_hbm,
                a_v, p_v, pt_v, z_v, w_v, stage, stage_y, sums, list_s, sem_a, sem_p, sem_w):
    capacity = hp_ref.shape[0]
    live = scal[0]
    first = scal[1]
    last = scal[2]

    p_copies = [pltpu.make_async_copy(p_hbm.at[pl.ds(u * SY, SY)], p_v.at[pl.ds(u * SY, SY)], sem_p.at[u])
                for u in range(SX)]
    for c in p_copies:
        c.start()

    def a_copy(k):
        at = pl.ds(pl.multiple_of(k * (CHUNK * B), CHUNK * B), CHUNK * B)
        return pltpu.make_async_copy(a_hbm.at[:, at], a_v.at[:, at], sem_a.at[k])

    used_chunks = (live + CHUNK - 1) // CHUNK

    @pl.loop(0, used_chunks)
    def _(k):
        a_copy(k).start()

    @functools.partial(lax.fori_loop, 0, 32, init_val=jnp.int32(0))
    def count(k, count):
        z_v[pl.ds(k * 24, 24)] = jnp.zeros((24, B, W2), f32)
        w_v[pl.ds(k * 5, 5)] = jnp.zeros((5, W2, W2), f32)
        for s in range(capacity // 32):
            h = hp_ref[k * (capacity // 32) + s]
            list_s[count] = h
            count = count + 1 + (h >> 31)
        return count

    for u in range(SX):
        p_copies[u].wait()
        for half in range(2):
            q = u * 2 + half
            flag = {0: first, SX - 1: last}.get(u)

            @pl.loop(0, PT_STEPS)
            def _(k):
                for s in range(16 // PT_STEPS):
                    t = k * (16 // PT_STEPS) + s
                    at = pl.ds(q * HALF + t * 2, 2)
                    pair = p_v[at]
                    if half == 1:
                        pair = swap_slots(pair) if flag is None else jnp.where(flag == 1, swap_slots(pair), pair)
                        p_v[at] = pair
                    pt_v[q * 16 + t] = pair.reshape(2 * B, W2).T

    for s in range(FAR):
        list_s[count + s] = jnp.int32(TRASH_W << 9)

    @pl.loop(0, used_chunks)
    def _(k):
        a_copy(k).wait()

    low = lanes_low(B)

    def far_dot(h):
        n = h >> 17
        par = (h >> 8) & 1
        r = h & 255
        a = a_v[:, pl.ds(pl.multiple_of((n >> 1) * W2, W2), W2)]
        a = jnp.where((n & 1) == par, a, swap_slots(a))
        a = jnp.where(low == (par == 0), a, jnp.zeros_like(a))
        even = (r & 1) == 0
        rhs = jnp.concatenate([jnp.where(even, a, jnp.zeros_like(a)),
                               jnp.where(even, jnp.zeros_like(a), a)], axis=0)
        return jnp.dot(pt_v[r >> 1], rhs, preferred_element_type=f32)

    @pl.loop(0, (count + FAR - 1) // FAR)
    def _(k):
        hs = [list_s[k * FAR + s] for s in range(FAR)]
        res = [far_dot(h) for h in hs]
        for s in range(0, FAR, 2):
            add_two(w_v, (hs[s] >> 9) & 255, (hs[s + 1] >> 9) & 255, res[s], res[s + 1])

    def w_copy(t):
        return pltpu.make_async_copy(
            stage.at[t], wt_hbm.at[t // 2, pl.ds((t % 2) * W2, W2)], sem_w.at[t])

    for t in range(4):
        @pl.loop(0, 32, unroll=8)
        def _(k):
            stage[t, :, pl.ds(pl.multiple_of(k * W2, W2), W2)] = w_v[t * 32 + k].astype(bf16)
        w_copy(t).start()

    @pl.loop(0, 32, unroll=8)
    def _(k):
        stage_y[:, pl.ds(pl.multiple_of(k * W2, W2), W2)] = w_v[N_WX + k].astype(bf16)

    y_copy = pltpu.make_async_copy(stage_y, wt_hbm.at[2, pl.ds(0, W2)], sem_w.at[4])
    y_copy.start()

    zero_p = jnp.zeros((B, W2), bf16)

    def near_dot(n):
        a = a_v[:, pl.ds(pl.multiple_of(n * B, W2), W2)]
        p0 = p_v[ci_ref[n]]
        p1 = p_v[ci_ref[n + 1]]
        w = jnp.concatenate([jnp.concatenate([p0, zero_p], axis=1),
                             jnp.concatenate([zero_p, p1], axis=1)], axis=0)
        return jnp.dot(a, w, preferred_element_type=f32)

    @pl.loop(0, (live + GROUP - 1) // GROUP)
    def _(g):
        n0 = g * GROUP
        res = {}
        for s in range(GROUP // 2 + DEPTH):
            if s < GROUP // 2:
                res[s] = near_dot(n0 + 2 * s)
            if s >= DEPTH:
                n, value = n0 + 2 * (s - DEPTH), res.pop(s - DEPTH)
                add_two(z_v, zi_ref[n], zi_ref[n + 1], value[:, :W2], value[:, W2:])

    low2 = lanes_low(W2)
    zb = jnp.zeros((B, W2), f32)
    for u in range(SX):
        mid = {0: first == 1, SX - 1: last == 1}.get(u)
        other = DN_AT if u == 0 else UP_AT
        for b in range(2):
            r0 = u * SY + b * HALF
            om = jnp.zeros((W2, W2), f32)
            oe = jnp.zeros((W2, 2 * W2), f32)
            for k in range(HALF // 4):
                r = r0 + 4 * k
                lhs = jnp.concatenate([pt_v[r // 2], pt_v[r // 2 + 1]], axis=1)
                zs = [z_v[pl.ds(g * FINE + r, 4)].reshape(4 * B, W2).astype(bf16) for g in range(3)]
                om += jnp.dot(lhs, zs[0], preferred_element_type=f32)
                oe += jnp.dot(lhs, jnp.concatenate(zs[1:], axis=1), preferred_element_type=f32)
            e0, e1 = oe[:, :W2], oe[:, W2:]
            same = om + jnp.where(low2, e0, roll(e1))
            adj = jnp.where(low2, roll(e0), e1)
            for g, c in ((1, same), (0 if u < 2 else 2, adj)):
                at = slice(g * W2, (g + 1) * W2)
                top, bot = c[:B], c[B:]
                if mid is not None:
                    slot = 0 if g == 1 else 1
                    sums[b * B:(b + 1) * B, other + slot * W2:other + (slot + 1) * W2] = jnp.where(mid, zb, bot)
                    bot = jnp.where(mid, bot, zb if b == 0 else top)
                    top = top if b == 0 else jnp.where(mid, top, zb)
                if b == 0 and (u == 0 or (u == 2 and g == 2)):
                    sums[:B, at] = top
                    sums[B:, at] = bot
                else:
                    sums[:B, at] += top
                    sums[B:, at] += bot

    out_copy = pltpu.make_async_copy(sums, sums_hbm.at[0], sem_w.at[5])
    out_copy.start()
    for t in range(4):
        w_copy(t).wait()
    y_copy.wait()
    out_copy.wait()


def tail_kernel(scal, sums_hbm, wt_hbm, yl_ref, yr_ref, hu_ref, hd_ref,
                own_ref, up_ref, dn_ref, sums, wy_ref, wt_ref, sem, sem_w):
    first, last, has_l, has_r = scal[1], scal[2], scal[3], scal[4]
    copies = [pltpu.make_async_copy(src, dst, sem.at[k]) for k, (src, dst) in enumerate(
        ((wt_hbm.at[2, pl.ds(0, W2)], wy_ref), (sums_hbm.at[0], sums)))]
    for c in copies:
        c.start()
    w_copies = [pltpu.make_async_copy(wt_hbm.at[t // 2, pl.ds((t % 2) * W2, W2)],
                                      wt_ref.at[t // 2, pl.ds((t % 2) * W2, W2)], sem_w.at[t]) for t in range(4)]
    for c in w_copies:
        c.start()

    low = lanes_low(W2)
    zl = jnp.zeros((B, W2), bf16)
    zt = jnp.zeros((W2, W2), f32)
    zb = jnp.zeros((B, W2), f32)
    rhs_y, is_mid = [], []
    for u in range(SX):
        mid = {0: first == 1, SX - 1: last == 1}.get(u)
        left = jnp.where(has_l == 1, yl_ref[u, 0], zl)
        right = jnp.where(has_r == 1, yr_ref[u, 0], zl)
        swapped = swap_slots(left)
        left = swapped if mid is None else jnp.where(mid, swapped, left)
        rhs_y.append(jnp.concatenate([jnp.concatenate([left, zl], axis=1),
                                      jnp.concatenate([zl, right], axis=1)], axis=0))
        is_mid.append(mid)
    for g in range(3):
        for k in (3 * g, 3 * g + 2):
            own_ref[:, k * W2:(k + 1) * W2] = zt

    copies[0].wait()
    for u in range(SX):
        mid = is_mid[u]
        other = dn_ref if u == 0 else up_ref
        for b in range(2):
            same = {-1: zt, 1: zt}
            adj = {-1: zt, 1: zt}
            for uc in range(max(0, u - 1), min(SX, u + 2)):
                k = uc * 8 + u * 2 + b
                ty = jnp.dot(wy_ref[:, k * W2:(k + 1) * W2], rhs_y[uc], preferred_element_type=f32)
                tl, tr = ty[:, :W2], ty[:, W2:]
                stays = is_mid[uc]
                if stays is None:
                    same[-1] += tl
                    same[1] += tr
                else:
                    same[-1] += jnp.where(stays, tl, jnp.where(low, zt, roll(tl)))
                    same[1] += jnp.where(stays, tr, jnp.where(low, tr, zt))
                    adj[-1] += jnp.where(stays, zt, jnp.where(low, zt, tl))
                    adj[1] += jnp.where(stays, zt, jnp.where(low, roll(tr), zt))
            adj_dx = 0 if u < 2 else 2
            for dy in (-1, 1):
                for dx, c in ((1, same[dy]), (adj_dx, adj[dy])):
                    at = slice((dx * 3 + dy + 1) * W2, (dx * 3 + dy + 2) * W2)
                    top, bot = c[:B], c[B:]
                    if mid is not None:
                        bot = jnp.where(mid, bot, zb if b == 0 else top)
                        top = top if b == 0 else jnp.where(mid, top, zb)
                    own_ref[:B, at] += top
                    own_ref[B:, at] += bot
            if mid is not None:
                q = slice(b * B, (b + 1) * B)
                for slot, c in ((2, same[-1]), (3, same[1]), (4, adj[-1] + adj[1])):
                    other[q, slot * W2:(slot + 1) * W2] = jnp.where(mid, zb, c[B:]).astype(bf16)

    for c in copies[1:]:
        c.wait()
    low2 = lanes_low(2 * W2)
    middle = [sums[:, dx * W2:(dx + 1) * W2] for dx in range(3)]
    for side, halo, valid, src, dst in ((0, hd_ref, first == 0, DN_AT, dn_ref), (1, hu_ref, last == 0, UP_AT, up_ref)):
        w_copies[2 * side].wait()
        w_copies[2 * side + 1].wait()
        t = []
        for b in range(2):
            rhs = halo[b * HALF:(b + 1) * HALF].reshape(HALF * B, W2)
            lhs = wt_ref[side, :, b * HALF * B:(b + 1) * HALF * B]
            out = jnp.dot(lhs, rhs, preferred_element_type=f32)
            t.append(jnp.where(valid, out, jnp.zeros_like(out)))
        same = jnp.where(low2, roll(t[0]), t[1])
        adj = jnp.where(low2, t[0], roll(t[1]))
        dx = 0 if side == 0 else 2
        middle[1] = middle[1] + jnp.concatenate([same[:B], same[W2:W2 + B]], axis=0)
        middle[dx] = middle[dx] + jnp.concatenate([adj[:B], adj[W2:W2 + B]], axis=0)
        away = [jnp.concatenate([x[B:W2], x[W2 + B:]], axis=0) for x in (same, adj)]
        for k in range(2):
            dst[:, k * W2:(k + 1) * W2] = (sums[:, src + k * W2:src + (k + 1) * W2] + away[k]).astype(bf16)
    for dx in range(3):
        own_ref[:, (3 * dx + 1) * W2:(3 * dx + 2) * W2] = middle[dx]


def edges_kernel(p_hbm, up_ref, dn_ref, yr_ref, yl_ref, sem):
    copies = [pltpu.make_async_copy(src, dst, sem.at[k]) for k, (src, dst) in enumerate((
        (p_hbm.at[SX - 1], up_ref), (p_hbm.at[0], dn_ref),
        (p_hbm.at[:, pl.ds(SY - 1, 1)], yr_ref), (p_hbm.at[:, pl.ds(0, 1)], yl_ref)))]
    for c in copies:
        c.start()
    for c in copies:
        c.wait()


def final_kernel(scal, own_ref, below_ref, above_ref, out_ref):
    low = lanes_low(W2)
    zero = jnp.zeros((W2, W2), f32)
    has_below = scal[1] == 0
    has_above = scal[2] == 0

    def piece(ref, k, valid):
        return jnp.where(valid, ref[:, k * W2:(k + 1) * W2].astype(f32), zero)

    lo = [piece(below_ref, k, has_below) for k in range(5)]
    hi = [piece(above_ref, k, has_above) for k in range(5)]
    sides = lo[4] + hi[4]
    extra = {
        0: lo[2], 1: lo[0], 2: lo[3],
        3: jnp.where(low, zero, sides), 4: lo[1] + hi[1], 5: jnp.where(low, sides, zero),
        6: hi[2], 7: hi[0], 8: hi[3],
    }
    for k, value in extra.items():
        out_ref[:, k * W2:(k + 1) * W2] = own_ref[:, k * W2:(k + 1) * W2] + value


def layout(rows, steps, cols, live, first, last):
    n = jnp.arange(rows.shape[0], dtype=jnp.int32)
    ur, br = rows // SY, (rows % SY) // HALF
    cx = ur + steps - 1
    outside = jnp.logical_or(cx < 0, cx >= SX)
    cy = jnp.where(outside, jnp.clip(cols - 1, 0, SY - 1), cols - 1)
    beside = jnp.logical_and(jnp.logical_not(outside), jnp.logical_or(cy < 0, cy >= SY))
    here = n < live
    far = jnp.logical_or(outside, beside)
    near = jnp.logical_and(here, jnp.logical_not(far))
    edge = jnp.logical_or(jnp.logical_and(cx == 0, first == 0), jnp.logical_and(cx == SX - 1, last == 0))
    kind = jnp.where(edge, 1 + cy // HALF, 0)
    ci = jnp.where(near, cx * SY + cy, 0)
    zi = jnp.where(near, kind * FINE + rows, TRASH_Z)
    side = (cx >= SX).astype(jnp.int32)
    y_side = (cy >= SY).astype(jnp.int32)
    wi = jnp.where(outside, (side * 2 + br) * HALF + cy // 2, N_WX + cx * 8 + ur * 2 + br)
    par = jnp.where(outside, cy % 2, y_side)
    hp = jnp.where(jnp.logical_and(here, far), (n << 17) | (wi << 9) | (par << 8) | rows, -1)
    return ci, zi, hp


def on_device(a_blocks, a_rows, a_steps, a_cols, a_live, p_blocks):
    capacity = a_rows.shape[2]
    n_row, n_col = lax.axis_size("row"), lax.axis_size("col")
    i, j = lax.axis_index("row"), lax.axis_index("col")

    def ring(x, axis, step):
        n = lax.axis_size(axis)
        return lax.ppermute(x, axis, [(k, (k + step) % n) for k in range(n)])

    smem = pl.BlockSpec(memory_space=pltpu.SMEM)
    vmem = pl.BlockSpec(memory_space=pltpu.VMEM)
    hbm = pl.BlockSpec(memory_space=pl.ANY)
    row = jax.ShapeDtypeStruct((SY, B, W2), bf16)
    column = jax.ShapeDtypeStruct((SX, 1, B, W2), bf16)
    p_last, p_first, p_right, p_left = pl.pallas_call(
        edges_kernel,
        in_specs=[hbm],
        out_specs=[vmem] * 4,
        out_shape=[row, row, column, column],
        scratch_shapes=[pltpu.SemaphoreType.DMA((4,))],
        compiler_params=pltpu.CompilerParams(vmem_limit_bytes=60 * MIB),
        name="edges",
    )(p_blocks)
    halo_dn = ring(p_last, "row", 1)
    halo_up = ring(p_first, "row", -1)
    y_left = ring(p_right, "col", 1)
    y_right = ring(p_left, "col", -1)

    live = a_live.reshape(())
    first = (i == 0).astype(jnp.int32)
    last = (i == n_row - 1).astype(jnp.int32)
    scal = jnp.stack([live, first, last, (j > 0).astype(jnp.int32), (j < n_col - 1).astype(jnp.int32)])
    ci, zi, hp = layout(a_rows.reshape(-1), a_steps.reshape(-1), a_cols.reshape(-1), live, first, last)

    sums, wt = pl.pallas_call(
        main_kernel,
        in_specs=[smem, smem, smem, smem, hbm, hbm],
        out_specs=[hbm, hbm],
        out_shape=[
            jax.ShapeDtypeStruct((SPARE_SUMS, W2, SUMS), f32),
            jax.ShapeDtypeStruct((SPARE_W, 2 * W2, SY * B), bf16),
        ],
        scratch_shapes=[
            pltpu.VMEM((B, capacity * B), bf16),
            pltpu.VMEM((FINE, B, W2), bf16),
            pltpu.VMEM((FINE // 2, W2, W2), bf16),
            pltpu.VMEM((TRASH_Z + 1, B, W2), f32),
            pltpu.VMEM((N_W + 1, W2, W2), f32),
            pltpu.VMEM((4, W2, SY * B), bf16),
            pltpu.VMEM((W2, 32 * W2), bf16),
            pltpu.VMEM((W2, SUMS), f32),
            pltpu.SMEM((capacity + FAR,), jnp.int32),
            pltpu.SemaphoreType.DMA((capacity // CHUNK,)),
            pltpu.SemaphoreType.DMA((SX,)),
            pltpu.SemaphoreType.DMA((6,)),
        ],
        compiler_params=pltpu.CompilerParams(vmem_limit_bytes=60 * MIB),
        cost_estimate=pl.CostEstimate(flops=4_000_000_000, bytes_accessed=20_000_000, transcendentals=0),
        name="galerkin_main",
    )(scal, ci, zi, hp, a_blocks.reshape(B, capacity * B), p_blocks.reshape(FINE, B, W2))

    own, up, dn = pl.pallas_call(
        tail_kernel,
        in_specs=[smem] + [hbm] * 2 + [vmem] * 4,
        out_specs=[vmem] * 3,
        out_shape=[
            jax.ShapeDtypeStruct((W2, 9 * W2), f32),
            jax.ShapeDtypeStruct((W2, 5 * W2), bf16),
            jax.ShapeDtypeStruct((W2, 5 * W2), bf16),
        ],
        scratch_shapes=[
            pltpu.VMEM((W2, SUMS), f32),
            pltpu.VMEM((W2, 32 * W2), bf16),
            pltpu.VMEM((2, 2 * W2, SY * B), bf16),
            pltpu.SemaphoreType.DMA((4,)),
            pltpu.SemaphoreType.DMA((4,)),
        ],
        compiler_params=pltpu.CompilerParams(vmem_limit_bytes=TAIL_VMEM * MIB),
        cost_estimate=pl.CostEstimate(flops=800_000_000, bytes_accessed=8_000_000, transcendentals=0),
        name="galerkin_halo",
    )(scal, sums, wt, y_left, y_right, halo_up, halo_dn)

    from_below = ring(up, "row", 1)
    from_above = ring(dn, "row", -1)

    return pl.pallas_call(
        final_kernel,
        in_specs=[smem] + [vmem] * 3,
        out_specs=vmem,
        out_shape=jax.ShapeDtypeStruct((W2, 9 * W2), f32),
        compiler_params=pltpu.CompilerParams(vmem_limit_bytes=8 * MIB),
        name="galerkin_sum",
    )(scal, own, from_below, from_above)


def solution(mesh):
    return jax.shard_map(
        on_device,
        mesh=mesh,
        in_specs=(
            P("row", "col", None, None),
            P("row", "col", None),
            P("row", "col", None),
            P("row", "col", None),
            P("row", "col"),
            P("row", "col", None, None),
        ),
        out_specs=P("row", "col"),
        check_vma=False,
    )
```

time: 436 us -> 55 us (0.13); the launches traced: 431 us -> 54.8 us
  local copies, waits for them, and re-layouts: 182 us -> 1.35 us
  matrix products: 161 us -> 0 us
  other arithmetic: 37.6 us -> 2.02 us
  Pallas kernels: 0 us -> 25.8 us
  waiting for transfers between devices: 33.1 us -> 9.59 us
    dot_general x8 -> x0, matrix products: 161 us -> none  [the longest x4 110 us: add_group(): jnp.einsum('nstrc,nsmtk->rmck', placing, contribs, precision=lax.Precisio...]
    dot_general x4 -> x0, local copies, waits for them, and re-layouts: 71.1 us -> none  [add_group(): jnp.einsum('nxa,nxb->nab', left_rows, product, preferred_element_type=jnp...]
    gather x8 -> x0, local copies, waits for them, and re-layouts: 47.7 us -> none  [the longest x4 24 us: add_group(): rows_table[lax.dynamic_slice_in_dim(row_cell, first_block, group_size, 0)]]
    add x9 -> x0, other arithmetic: 26.9 us -> none  [the longest x4 24 us: add_group(): partial_value + jnp.einsum('nstrc,nsmtk->rmck', placing, contribs, precis...]
    pallas_call x0 -> x4, Pallas kernels: none -> 25.8 us  [the longest x1 16.7 us: on_device(): pl.pallas_call(main_kernel, in_specs=[smem, smem, smem, smem, hbm, hbm],...]
    ppermute x6, waiting for transfers between devices: 33.1 us -> 9.59 us  [ring(): return lax.ppermute(x, axis, [(k, (k + step) % n) for k in range(n)])]
    dynamic_slice x8 -> x0, local copies, waits for them, and re-layouts: 18.5 us -> none  [the longest x4 18.5 us: add_group(): a_piece = lax.dynamic_slice_in_dim(matrix, first_block, group_size, 1)]
    reshape x1 -> x0, local copies, waits for them, and re-layouts: 18.1 us -> none  [on_device(): matrix = a_blocks.reshape(block_size, capacity, block_size)]
  transfers between devices with their start and end apart: 6 -> 6, of which waited for: 4 -> 3; matrix products, arithmetic and copies ran while one was open for 7% -> 5% of each run, Pallas kernels for 0% -> 31%
where the time goes in v1:
time: 55 us; the launch traced here: 54.8 us
  Pallas kernels  25.8 us (47%)
  starting transfers between devices  15.3 us (28%)
  waiting for transfers between devices  9.59 us (17%)
  other arithmetic  2.02 us (4%)
  local copies, waits for them, and re-layouts  1.35 us (2%)
  between operations  0.71 us (1%)
    pallas_call x1, Pallas kernels, on_device(): pl.pallas_call(main_kernel, in_specs=[smem, smem, smem, smem, hbm, hbm],...  16.7 us
    ppermute x6, starting transfers between devices, ring(): return lax.ppermute(x, axis, [(k, (k + step) % n) for k in range(n)])  15.3 us
    ppermute x6, waiting for transfers between devices, ring(): return lax.ppermute(x, axis, [(k, (k + step) % n) for k in range(n)])  9.59 us
    pallas_call x1, Pallas kernels, on_device(): pl.pallas_call(tail_kernel, in_specs=[smem] + [hbm] * 2 + [vmem] * 4, out...  4.72 us
    pallas_call x1, Pallas kernels, on_device(): pl.pallas_call(edges_kernel, in_specs=[hbm], out_specs=[vmem] * 4, out_sh...  2.92 us
    pallas_call x1, Pallas kernels, on_device(): pl.pallas_call(final_kernel, in_specs=[smem] + [vmem] * 3, out_specs=vmem...  1.43 us
    select_n x1, other arithmetic, layout(): jnp.where(jnp.logical_and(here, far), n << 17 | wi << 9 | par << 8 | rows...  1.33 us
  transfers between devices with their start and end apart: 6, of which 3 were waited for; matrix products, arithmetic and copies ran while one was open for 5% of the time, Pallas kernels for 31%

profile of v1, /device:TPU:16, one launch (start us, length us, event | category | flops | bytes accessed | tf_op | source)
XLA Modules:
  0.0 54.8 jit_solution(2730041680099701601)
XLA Ops:
  0.0 2.9 %edges.1 = (bf16[64,64,128]{2,1,0:T(8,128)(2,1)}, bf16[64,64,128]{2,1,0:T(8,128)(2,1)}, bf16[4,1,64,128]{3,2,1,0:T(8,128)(2,1)}, bf16[4,1,64,128]{3,2,1,0:T(8,128)(2,1)}) custom-call(bf16[4,64,64,128]{3,2,1,0:T(8,128)(2,1)} %p_hbm.1), custom_call_target="tpu_custom_call" | custom-call | tf_op jit(solution)/shard_map/edges/pallas_call | solution.py:364
  2.9 8.1 %collective-permute-start.2 = (bf16[64,64,128]{2,1,0:T(8,128)(2,1)}, bf16[64,64,128]{2,1,0:T(8,128)(2,1)S(1)}, u32[]{:S(2)}, u32[]{:S(2)}) collective-permute-start(bf16[64,64,128]{2,1,0:T(8,128)(2,1)} %get-tuple-element.18), channel_id=1, source_target_pairs={{0,248},{8,0},{16,8},{24,16},{32,24},{40,32},{48,40},{56,48},{64,5... | collective-permute-start | bytes 3145736 | tf_op jit(solution)/shard_map/ppermute | solution.py:357
  11.1 0.0 collective-permute-start.3
  11.1 0.0 collective-permute-start
  11.1 1.7 %collective-permute-start.1 = (bf16[4,1,64,128]{3,2,1,0:T(8,128)(2,1)}, bf16[4,1,64,128]{3,2,1,0:T(8,128)(2,1)S(1)}, u32[]{:S(2)}, u32[]{:S(2)}) collective-permute-start(bf16[4,1,64,128]{3,2,1,0:T(8,128)(2,1)} %get-tuple-element.17), channel_id=1, source_target_pairs={{0,7},{1,0},{2,1},{3,2},{4,3},{5,4},{6,5},{7,6},{8,15},{9,8},{10,9... | collective-permute-start | bytes 196616 | tf_op jit(solution)/shard_map/ppermute | solution.py:357
  13.5 0.7 %stack.27.scal = s32[5]{0:T(128)} concatenate(s32[1]{0:T(128)} %bitcast.11, s32[1]{0:T(128)} %bitcast.1, s32[1]{0:T(128)} %bitcast.2, s32[1]{0:T(128)} %bitcast.3, s32[1]{0:T(128)} %bitcast.4), dimensions={0} | concatenate | bytes 40 | tf_op jit(solution)/shard_map/stack | solution.py:381
  14.1 0.7 %broadcast_add_fusion = s32[1,1,1024]{2,1,0:T(1,128)S(1)} fusion(s32[1,1,1024]{2,1,0:T(1,128)} %param.9), kind=kLoop, calls=%fused_computation.54 | loop fusion | flops 1024 | bytes 8192 | tf_op jit(solution)/shard_map/sub | solution.py:333
  14.8 1.3 %fusion.13 = (s32[1024]{0:T(1024)}, s32[1024]{0:T(1024)}, s32[1024]{0:T(1024)}) fusion(s32[1024]{0:T(1024)} %bitcast.15, s32[1024]{0:T(1024)S(1)} %bitcast.14, s32[]{:T(128)} %bitcast.12, s32[1024]{0:T(1024)} %bitcast.16, pred[]{:T(512)S(6)} %eq.30, pred[]{:T(512)S(6)} %eq.27), kind=kLoop, calls=%fused_computation.31 | loop fusion | flops 113664 | bytes 24582 | tf_op jit(solution)/shard_map/jit(_where)/select_n | solution.py:346
  16.2 16.7 %galerkin_main.1 = (f32[144,128,896]{2,1,0:T(8,128)}, bf16[32,256,4096]{2,1,0:T(8,128)(2,1)}) custom-call(s32[5]{0:T(128)} %stack.27.scal, s32[1024]{0:T(1024)} %get-tuple-element.25.ci_ref, s32[1024]{0:T(1024)} %get-tuple-element.24.zi_ref, s32[1024]{0:T(1024)} %get-tuple-element.23.hp_ref, bf16[64,65536]{1,0:T(8,128)(2,1)} %bitcast.17, ...), custom_call_target="tpu_custom_call" | custom-call | flops 4000000000 | bytes 20000000 | tf_op jit(solution)/shard_map/galerkin_main/pallas_call | solution.py:384
  32.9 0.0 collective-permute-done.yl_ref
  32.9 0.0 collective-permute-done.1.yr_ref
  32.9 0.9 %collective-permute-done.2.hu_ref = bf16[64,64,128]{2,1,0:T(8,128)(2,1)S(1)} collective-permute-done((bf16[64,64,128]{2,1,0:T(8,128)(2,1)}, bf16[64,64,128]{2,1,0:T(8,128)(2,1)S(1)}, u32[]{:S(2)}, u32[]{:S(2)}) %collective-permute-start.2) | collective-permute-done | bytes 1048608 | tf_op jit(solution)/shard_map/ppermute | solution.py:357
  33.8 5.4 %collective-permute-done.3.hd_ref = bf16[64,64,128]{2,1,0:T(8,128)(2,1)S(1)} collective-permute-done((bf16[64,64,128]{2,1,0:T(8,128)(2,1)}, bf16[64,64,128]{2,1,0:T(8,128)(2,1)S(1)}, u32[]{:S(2)}, u32[]{:S(2)}) %collective-permute-start.3) | collective-permute-done | bytes 1048608 | tf_op jit(solution)/shard_map/ppermute | solution.py:357
  39.2 0.0 copy-start
  39.2 0.7 %copy-done = s32[5]{0:T(128)S(1)} copy-done((s32[5]{0:T(128)S(1)}, s32[5]{0:T(128)}, u32[]{:S(2)}) %copy-start) | copy-done | bytes 44
  39.9 4.7 %galerkin_halo.1 = (f32[128,1152]{1,0:T(8,128)S(1)}, bf16[128,640]{1,0:T(8,128)(2,1)S(1)}, bf16[128,640]{1,0:T(8,128)(2,1)S(1)}) custom-call(s32[5]{0:T(128)S(1)} %copy-done, f32[144,128,896]{2,1,0:T(8,128)} %get-tuple-element.14.sums_hbm, bf16[32,256,4096]{2,1,0:T(8,128)(2,1)} %get-tuple-element.15.wt_hbm, ...), custom_call_target="tpu_custom_call" | custom-call | flops 800000000 | bytes 8000000 | tf_op jit(solution)/shard_map/galerkin_halo/pallas_call | solution.py:411
  44.6 0.1 collective-permute-start.4
  44.7 5.3 %collective-permute-start.5 = (bf16[128,640]{1,0:T(8,128)(2,1)S(1)}, bf16[128,640]{1,0:T(8,128)(2,1)S(1)}, u32[]{:S(2)}, u32[]{:S(2)}) collective-permute-start(bf16[128,640]{1,0:T(8,128)(2,1)S(1)} %get-tuple-element.22), channel_id=1, source_target_pairs={{0,248},{8,0},{16,8},{24,16},{32,24},{40,32},{48,40},{56,48},{64,5... | collective-permute-start | bytes 491528 | tf_op jit(solution)/shard_map/ppermute | solution.py:357
  50.0 3.3 %collective-permute-done.4.below_ref = bf16[128,640]{1,0:T(8,128)(2,1)S(1)} collective-permute-done((bf16[128,640]{1,0:T(8,128)(2,1)S(1)}, bf16[128,640]{1,0:T(8,128)(2,1)S(1)}, u32[]{:S(2)}, u32[]{:S(2)}) %collective-permute-start.4) | collective-permute-done | bytes 163872 | tf_op jit(solution)/shard_map/ppermute | solution.py:357
  53.3 0.0 collective-permute-done.5.above_ref
  53.3 1.4 %galerkin_sum.1 = f32[128,1152]{1,0:T(8,128)} custom-call(s32[5]{0:T(128)S(1)} %copy-done, f32[128,1152]{1,0:T(8,128)S(1)} %get-tuple-element.20.own_ref, bf16[128,640]{1,0:T(8,128)(2,1)S(1)} %collective-permute-done.4.below_ref, bf16[128,640]{1,0:T(8,128)(2,1)S(1)} %collective-permute-done.5.above_ref), custom_call_target="tpu_custom_call" | custom-call | tf_op jit(solution)/shard_map/galerkin_sum/pallas_call | solution.py:435
Async XLA Ops:
  2.9 30.9 %collective-permute-start.2 = (bf16[64,64,128]{2,1,0:T(8,128)(2,1)}, bf16[64,64,128]{2,1,0:T(8,128)(2,1)S(1)}, u32[]{:S(2)}, u32[]{:S(2)}) collective-permute-start(bf16[64,64,128]{2,1,0:T(8,128)(2,1)} %get-tuple-element.18), channel_id=1, source_target_pairs={{0,248},{8,0},{16,8},{24,16},{32,24},{40,32},{48,40},{56,48},{64,5... | collective-permute-start | bytes 3145736 | tf_op jit(solution)/shard_map/ppermute | solution.py:357
  11.1 28.1 %collective-permute-start.3 = (bf16[64,64,128]{2,1,0:T(8,128)(2,1)}, bf16[64,64,128]{2,1,0:T(8,128)(2,1)S(1)}, u32[]{:S(2)}, u32[]{:S(2)}) collective-permute-start(bf16[64,64,128]{2,1,0:T(8,128)(2,1)} %get-tuple-element.19), channel_id=1, source_target_pairs={{0,8},{8,16},{16,24},{24,32},{32,40},{40,48},{48,56},{56,64},{64,7... | collective-permute-start | bytes 3145736 | tf_op jit(solution)/shard_map/ppermute | solution.py:357
  11.1 21.8 %collective-permute-start = (bf16[4,1,64,128]{3,2,1,0:T(8,128)(2,1)}, bf16[4,1,64,128]{3,2,1,0:T(8,128)(2,1)S(1)}, u32[]{:S(2)}, u32[]{:S(2)}) collective-permute-start(bf16[4,1,64,128]{3,2,1,0:T(8,128)(2,1)} %get-tuple-element.16), channel_id=1, source_target_pairs={{0,1},{1,2},{2,3},{3,4},{4,5},{5,6},{6,7},{7,0},{8,9},{9,10},{10,1... | collective-permute-start | bytes 196616 | tf_op jit(solution)/shard_map/ppermute | solution.py:357
  11.1 21.8 %collective-permute-start.1 = (bf16[4,1,64,128]{3,2,1,0:T(8,128)(2,1)}, bf16[4,1,64,128]{3,2,1,0:T(8,128)(2,1)S(1)}, u32[]{:S(2)}, u32[]{:S(2)}) collective-permute-start(bf16[4,1,64,128]{3,2,1,0:T(8,128)(2,1)} %get-tuple-element.17), channel_id=1, source_target_pairs={{0,7},{1,0},{2,1},{3,2},{4,3},{5,4},{6,5},{7,6},{8,15},{9,8},{10,9... | collective-permute-start | bytes 196616 | tf_op jit(solution)/shard_map/ppermute | solution.py:357
  39.2 0.7 %copy-start = (s32[5]{0:T(128)S(1)}, s32[5]{0:T(128)}, u32[]{:S(2)}) copy-start(s32[5]{0:T(128)} %stack.27.scal) | copy-start | bytes 64
  44.6 8.7 %collective-permute-start.4 = (bf16[128,640]{1,0:T(8,128)(2,1)S(1)}, bf16[128,640]{1,0:T(8,128)(2,1)S(1)}, u32[]{:S(2)}, u32[]{:S(2)}) collective-permute-start(bf16[128,640]{1,0:T(8,128)(2,1)S(1)} %get-tuple-element.21), channel_id=1, source_target_pairs={{0,8},{8,16},{16,24},{24,32},{32,40},{40,48},{48,56},{56,64},{64,7... | collective-permute-start | bytes 491528 | tf_op jit(solution)/shard_map/ppermute | solution.py:357
  44.7 8.6 %collective-permute-start.5 = (bf16[128,640]{1,0:T(8,128)(2,1)S(1)}, bf16[128,640]{1,0:T(8,128)(2,1)S(1)}, u32[]{:S(2)}, u32[]{:S(2)}) collective-permute-start(bf16[128,640]{1,0:T(8,128)(2,1)S(1)} %get-tuple-element.22), channel_id=1, source_target_pairs={{0,248},{8,0},{16,8},{24,16},{32,24},{40,32},{48,40},{56,48},{64,5... | collective-permute-start | bytes 491528 | tf_op jit(solution)/shard_map/ppermute | solution.py:357

commit v2 on v1

--- a/solution.py
+++ b/solution.py
@@ -36,6 +36,11 @@
     return lax.broadcasted_iota(jnp.int32, (rows, W2), 1) < B
 
 
+def place(axis):
+    i = lax.axis_index(axis)
+    return i == 0, i == lax.axis_size(axis) - 1, i % 2 == 0
+
+
 def roll(x):
     return pltpu.roll(x, B, 1)
 
@@ -47,13 +52,12 @@
     ref[j] = jnp.where(i == j, new_i, old_j) + y
 
 
-def main_kernel(scal, ci_ref, zi_ref, hp_ref, a_hbm, p_hbm,
+def main_kernel(live_ref, ci_ref, zi_ref, hp_ref, a_hbm, p_hbm,
                 sums_hbm, wt_hbm,
                 a_v, p_v, pt_v, z_v, w_v, stage, stage_y, sums, list_s, sem_a, sem_p, sem_w):
     capacity = hp_ref.shape[0]
-    live = scal[0]
-    first = scal[1]
-    last = scal[2]
+    live = live_ref[0, 0]
+    first, last, _ = place("row")
 
     p_copies = [pltpu.make_async_copy(p_hbm.at[pl.ds(u * SY, SY)], p_v.at[pl.ds(u * SY, SY)], sem_p.at[u])
                 for u in range(SX)]
@@ -93,7 +97,7 @@
                     at = pl.ds(q * HALF + t * 2, 2)
                     pair = p_v[at]
                     if half == 1:
-                        pair = swap_slots(pair) if flag is None else jnp.where(flag == 1, swap_slots(pair), pair)
+                        pair = swap_slots(pair) if flag is None else jnp.where(flag, swap_slots(pair), pair)
                         p_v[at] = pair
                     pt_v[q * 16 + t] = pair.reshape(2 * B, W2).T
 
@@ -166,7 +170,7 @@
     low2 = lanes_low(W2)
     zb = jnp.zeros((B, W2), f32)
     for u in range(SX):
-        mid = {0: first == 1, SX - 1: last == 1}.get(u)
+        mid = {0: first, SX - 1: last}.get(u)
         other = DN_AT if u == 0 else UP_AT
         for b in range(2):
             r0 = u * SY + b * HALF
@@ -204,9 +208,10 @@
     out_copy.wait()
 
 
-def tail_kernel(scal, sums_hbm, wt_hbm, yl_ref, yr_ref, hu_ref, hd_ref,
-                own_ref, up_ref, dn_ref, sums, wy_ref, wt_ref, sem, sem_w):
-    first, last, has_l, has_r = scal[1], scal[2], scal[3], scal[4]
+def beside_kernel(sums_hbm, wt_hbm, yl_ref, yr_ref,
+                  own_ref, up_ref, dn_ref, wt_ref, sums, wy_ref, sem, sem_w):
+    first, last, _ = place("row")
+    no_l, no_r, _ = place("col")
     copies = [pltpu.make_async_copy(src, dst, sem.at[k]) for k, (src, dst) in enumerate(
         ((wt_hbm.at[2, pl.ds(0, W2)], wy_ref), (sums_hbm.at[0], sums)))]
     for c in copies:
@@ -222,9 +227,9 @@
     zb = jnp.zeros((B, W2), f32)
     rhs_y, is_mid = [], []
     for u in range(SX):
-        mid = {0: first == 1, SX - 1: last == 1}.get(u)
-        left = jnp.where(has_l == 1, yl_ref[u, 0], zl)
-        right = jnp.where(has_r == 1, yr_ref[u, 0], zl)
+        mid = {0: first, SX - 1: last}.get(u)
+        left = jnp.where(no_l, zl, yl_ref[u, 0])
+        right = jnp.where(no_r, zl, yr_ref[u, 0])
         swapped = swap_slots(left)
         left = swapped if mid is None else jnp.where(mid, swapped, left)
         rhs_y.append(jnp.concatenate([jnp.concatenate([left, zl], axis=1),
@@ -267,36 +272,56 @@
             if mid is not None:
                 q = slice(b * B, (b + 1) * B)
                 for slot, c in ((2, same[-1]), (3, same[1]), (4, adj[-1] + adj[1])):
-                    other[q, slot * W2:(slot + 1) * W2] = jnp.where(mid, zb, c[B:]).astype(bf16)
-
-    for c in copies[1:]:
+                    other[q, slot * W2:(slot + 1) * W2] = jnp.where(mid, zb, c[B:])
+
+    copies[1].wait()
+    for dx in range(3):
+        own_ref[:, (3 * dx + 1) * W2:(3 * dx + 2) * W2] = sums[:, dx * W2:(dx + 1) * W2]
+    up_ref[:, :2 * W2] = sums[:, UP_AT:DN_AT]
+    dn_ref[:, :2 * W2] = sums[:, DN_AT:]
+    for c in w_copies:
         c.wait()
-    low2 = lanes_low(2 * W2)
-    middle = [sums[:, dx * W2:(dx + 1) * W2] for dx in range(3)]
-    for side, halo, valid, src, dst in ((0, hd_ref, first == 0, DN_AT, dn_ref), (1, hu_ref, last == 0, UP_AT, up_ref)):
-        w_copies[2 * side].wait()
-        w_copies[2 * side + 1].wait()
+
+
+def tail_kernel(own_in, up_in, dn_in, wt_ref, ha_ref, hb_ref, own_ref, oa_ref, ob_ref):
+    first, last, even = place("row")
+    low = lanes_low(2 * W2)
+    middle = [own_in[:, (3 * dx + 1) * W2:(3 * dx + 2) * W2] for dx in range(3)]
+    away = []
+    for side, valid, src in ((0, jnp.logical_not(first), dn_in), (1, jnp.logical_not(last), up_in)):
         t = []
         for b in range(2):
-            rhs = halo[b * HALF:(b + 1) * HALF].reshape(HALF * B, W2)
+            near = slice(b * HALF, (b + 1) * HALF)
+            one, two = (ha_ref, hb_ref) if side == 1 else (hb_ref, ha_ref)
+            rhs = jnp.where(even, one[near], two[near]).reshape(HALF * B, W2)
             lhs = wt_ref[side, :, b * HALF * B:(b + 1) * HALF * B]
             out = jnp.dot(lhs, rhs, preferred_element_type=f32)
             t.append(jnp.where(valid, out, jnp.zeros_like(out)))
-        same = jnp.where(low2, roll(t[0]), t[1])
-        adj = jnp.where(low2, t[0], roll(t[1]))
+        same = jnp.where(low, roll(t[0]), t[1])
+        adj = jnp.where(low, t[0], roll(t[1]))
         dx = 0 if side == 0 else 2
         middle[1] = middle[1] + jnp.concatenate([same[:B], same[W2:W2 + B]], axis=0)
         middle[dx] = middle[dx] + jnp.concatenate([adj[:B], adj[W2:W2 + B]], axis=0)
-        away = [jnp.concatenate([x[B:W2], x[W2 + B:]], axis=0) for x in (same, adj)]
-        for k in range(2):
-            dst[:, k * W2:(k + 1) * W2] = (sums[:, src + k * W2:src + (k + 1) * W2] + away[k]).astype(bf16)
+        parts = [src[:, k * W2:(k + 1) * W2] for k in range(5)]
+        for k, x in enumerate((same, adj)):
+            parts[k] = parts[k] + jnp.concatenate([x[B:W2], x[W2 + B:]], axis=0)
+        away.append(parts)
+    for k in range(5):
+        at = slice(k * W2, (k + 1) * W2)
+        oa_ref[:, at] = jnp.where(even, away[1][k], away[0][k]).astype(bf16)
+        ob_ref[:, at] = jnp.where(even, away[0][k], away[1][k]).astype(bf16)
     for dx in range(3):
         own_ref[:, (3 * dx + 1) * W2:(3 * dx + 2) * W2] = middle[dx]
-
-
-def edges_kernel(p_hbm, up_ref, dn_ref, yr_ref, yl_ref, sem):
+        for dy in (0, 2):
+            at = slice((3 * dx + dy) * W2, (3 * dx + dy + 1) * W2)
+            own_ref[:, at] = own_in[:, at]
+
+
+def edges_kernel(p_hbm, xa_ref, xb_ref, yr_ref, yl_ref, sem):
+    _, _, even = place("row")
+    to_a = jnp.where(even, SX - 1, 0)
     copies = [pltpu.make_async_copy(src, dst, sem.at[k]) for k, (src, dst) in enumerate((
-        (p_hbm.at[SX - 1], up_ref), (p_hbm.at[0], dn_ref),
+        (p_hbm.at[to_a], xa_ref), (p_hbm.at[SX - 1 - to_a], xb_ref),
         (p_hbm.at[:, pl.ds(SY - 1, 1)], yr_ref), (p_hbm.at[:, pl.ds(0, 1)], yl_ref)))]
     for c in copies:
         c.start()
@@ -304,17 +329,14 @@
         c.wait()
 
 
-def final_kernel(scal, own_ref, below_ref, above_ref, out_ref):
+def final_kernel(own_ref, ra_ref, rb_ref, out_ref):
+    first, last, even = place("row")
     low = lanes_low(W2)
     zero = jnp.zeros((W2, W2), f32)
-    has_below = scal[1] == 0
-    has_above = scal[2] == 0
-
-    def piece(ref, k, valid):
-        return jnp.where(valid, ref[:, k * W2:(k + 1) * W2].astype(f32), zero)
-
-    lo = [piece(below_ref, k, has_below) for k in range(5)]
-    hi = [piece(above_ref, k, has_above) for k in range(5)]
+    a = [ra_ref[:, k * W2:(k + 1) * W2].astype(f32) for k in range(5)]
+    b = [rb_ref[:, k * W2:(k + 1) * W2].astype(f32) for k in range(5)]
+    lo = [jnp.where(first, zero, jnp.where(even, y, x)) for x, y in zip(a, b)]
+    hi = [jnp.where(last, zero, jnp.where(even, x, y)) for x, y in zip(a, b)]
     sides = lo[4] + hi[4]
     extra = {
         0: lo[2], 1: lo[0], 2: lo[3],
@@ -349,36 +371,38 @@
 
 def on_device(a_blocks, a_rows, a_steps, a_cols, a_live, p_blocks):
     capacity = a_rows.shape[2]
-    n_row, n_col = lax.axis_size("row"), lax.axis_size("col")
-    i, j = lax.axis_index("row"), lax.axis_index("col")
+    n_row = lax.axis_size("row")
+    i = lax.axis_index("row")
 
     def ring(x, axis, step):
         n = lax.axis_size(axis)
         return lax.ppermute(x, axis, [(k, (k + step) % n) for k in range(n)])
+
+    pairs_a = [(k, min(k ^ 1, n_row - 1)) for k in range(n_row)]
+    pairs_b = [(k, min(max(((k + 1) ^ 1) - 1, 0), n_row - 1)) for k in range(n_row)]
 
     smem = pl.BlockSpec(memory_space=pltpu.SMEM)
     vmem = pl.BlockSpec(memory_space=pltpu.VMEM)
     hbm = pl.BlockSpec(memory_space=pl.ANY)
     row = jax.ShapeDtypeStruct((SY, B, W2), bf16)
     column = jax.ShapeDtypeStruct((SX, 1, B, W2), bf16)
-    p_last, p_first, p_right, p_left = pl.pallas_call(
+    x_a, x_b, p_right, p_left = pl.pallas_call(
         edges_kernel,
         in_specs=[hbm],
-        out_specs=[vmem] * 4,
+        out_specs=[hbm] * 4,
         out_shape=[row, row, column, column],
         scratch_shapes=[pltpu.SemaphoreType.DMA((4,))],
-        compiler_params=pltpu.CompilerParams(vmem_limit_bytes=60 * MIB),
+        compiler_params=pltpu.CompilerParams(vmem_limit_bytes=52 * MIB),
         name="edges",
     )(p_blocks)
-    halo_dn = ring(p_last, "row", 1)
-    halo_up = ring(p_first, "row", -1)
+    halo_a = lax.ppermute(x_a, "row", pairs_a)
+    halo_b = lax.ppermute(x_b, "row", pairs_b)
     y_left = ring(p_right, "col", 1)
     y_right = ring(p_left, "col", -1)
 
     live = a_live.reshape(())
     first = (i == 0).astype(jnp.int32)
     last = (i == n_row - 1).astype(jnp.int32)
-    scal = jnp.stack([live, first, last, (j > 0).astype(jnp.int32), (j < n_col - 1).astype(jnp.int32)])
     ci, zi, hp = layout(a_rows.reshape(-1), a_steps.reshape(-1), a_cols.reshape(-1), live, first, last)
 
     sums, wt = pl.pallas_call(
@@ -406,40 +430,52 @@
         compiler_params=pltpu.CompilerParams(vmem_limit_bytes=60 * MIB),
         cost_estimate=pl.CostEstimate(flops=4_000_000_000, bytes_accessed=20_000_000, transcendentals=0),
         name="galerkin_main",
-    )(scal, ci, zi, hp, a_blocks.reshape(B, capacity * B), p_blocks.reshape(FINE, B, W2))
-
-    own, up, dn = pl.pallas_call(
-        tail_kernel,
-        in_specs=[smem] + [hbm] * 2 + [vmem] * 4,
-        out_specs=[vmem] * 3,
+    )(a_live, ci, zi, hp, a_blocks.reshape(B, capacity * B), p_blocks.reshape(FINE, B, W2))
+
+    own_shape = jax.ShapeDtypeStruct((W2, 9 * W2), f32)
+    own, up, dn, wt = pl.pallas_call(
+        beside_kernel,
+        in_specs=[hbm] * 2 + [vmem] * 2,
+        out_specs=[vmem] * 4,
         out_shape=[
-            jax.ShapeDtypeStruct((W2, 9 * W2), f32),
-            jax.ShapeDtypeStruct((W2, 5 * W2), bf16),
-            jax.ShapeDtypeStruct((W2, 5 * W2), bf16),
+            own_shape,
+            jax.ShapeDtypeStruct((W2, 5 * W2), f32),
+            jax.ShapeDtypeStruct((W2, 5 * W2), f32),
+            jax.ShapeDtypeStruct((2, 2 * W2, SY * B), bf16),
         ],
         scratch_shapes=[
             pltpu.VMEM((W2, SUMS), f32),
             pltpu.VMEM((W2, 32 * W2), bf16),
-            pltpu.VMEM((2, 2 * W2, SY * B), bf16),
-            pltpu.SemaphoreType.DMA((4,)),
+            pltpu.SemaphoreType.DMA((2,)),
             pltpu.SemaphoreType.DMA((4,)),
         ],
         compiler_params=pltpu.CompilerParams(vmem_limit_bytes=TAIL_VMEM * MIB),
-        cost_estimate=pl.CostEstimate(flops=800_000_000, bytes_accessed=8_000_000, transcendentals=0),
+        cost_estimate=pl.CostEstimate(flops=200_000_000, bytes_accessed=10_000_000, transcendentals=0),
+        name="galerkin_beside",
+    )(sums, wt, y_left, y_right)
+
+    sent = jax.ShapeDtypeStruct((W2, 5 * W2), bf16)
+    own, to_a, to_b = pl.pallas_call(
+        tail_kernel,
+        in_specs=[vmem] * 6,
+        out_specs=[vmem] * 3,
+        out_shape=[own_shape, sent, sent],
+        compiler_params=pltpu.CompilerParams(vmem_limit_bytes=TAIL_VMEM * MIB),
+        cost_estimate=pl.CostEstimate(flops=600_000_000, bytes_accessed=8_000_000, transcendentals=0),
         name="galerkin_halo",
-    )(scal, sums, wt, y_left, y_right, halo_up, halo_dn)
-
-    from_below = ring(up, "row", 1)
-    from_above = ring(dn, "row", -1)
+    )(own, up, dn, wt, halo_a, halo_b)
+
+    from_a = lax.ppermute(to_a, "row", pairs_a)
+    from_b = lax.ppermute(to_b, "row", pairs_b)
 
     return pl.pallas_call(
         final_kernel,
-        in_specs=[smem] + [vmem] * 3,
+        in_specs=[vmem] * 3,
         out_specs=vmem,
-        out_shape=jax.ShapeDtypeStruct((W2, 9 * W2), f32),
+        out_shape=own_shape,
         compiler_params=pltpu.CompilerParams(vmem_limit_bytes=8 * MIB),
         name="galerkin_sum",
-    )(scal, own, from_below, from_above)
+    )(own, from_a, from_b)
 
 
 def solution(mesh):

time: 55 us -> 81.1 us (1.47)
  the two profiles are of different devices: /device:TPU:16 before, /device:TPU:6 now
where the time goes in v2:
time: 81.1 us; the launch traced here: 79.5 us
  Pallas kernels  55.2 us (68%)
  starting transfers between devices  15.6 us (19%)
  waiting for transfers between devices  5.94 us (7%)
  other arithmetic  2.02 us (2%)
    pallas_call x1, Pallas kernels, on_device(): pl.pallas_call(edges_kernel, in_specs=[hbm], out_specs=[hbm] * 4, out_sha...  32.9 us
    pallas_call x1, Pallas kernels, on_device(): pl.pallas_call(main_kernel, in_specs=[smem, smem, smem, smem, hbm, hbm],...  17.2 us
    ppermute x1, starting transfers between devices, on_device(): halo_b = lax.ppermute(x_b, 'row', pairs_b)  7.11 us
    ppermute x1, waiting for transfers between devices, on_device(): from_b = lax.ppermute(to_b, 'row', pairs_b)  4.02 us
    ppermute x1, starting transfers between devices, on_device(): from_b = lax.ppermute(to_b, 'row', pairs_b)  3.39 us
    ppermute x2, starting transfers between devices, ring(): return lax.ppermute(x, axis, [(k, (k + step) % n) for k in range(n)])  2.96 us
    pallas_call x1, Pallas kernels, on_device(): pl.pallas_call(beside_kernel, in_specs=[hbm] * 2 + [vmem] * 2, out_specs=...  2.69 us
    ppermute x1, starting transfers between devices, on_device(): halo_a = lax.ppermute(x_a, 'row', pairs_a)  2 us
  transfers between devices with their start and end apart: 6, of which 2 were waited for; matrix products, arithmetic and copies ran while one was open for 3% of the time, Pallas kernels for 25%

profile of v2, /device:TPU:6, one launch (start us, length us, event | category | flops | bytes accessed | tf_op | source)
XLA Modules:
  0.0 79.5 jit_solution(9078440513380934607)
XLA Ops:
  0.0 32.9 %edges.1 = (bf16[64,64,128]{2,1,0:T(8,128)(2,1)S(1)}, bf16[64,64,128]{2,1,0:T(8,128)(2,1)}, bf16[4,1,64,128]{3,2,1,0:T(8,128)(2,1)S(1)}, bf16[4,1,64,128]{3,2,1,0:T(8,128)(2,1)S(1)}) custom-call(bf16[4,64,64,128]{3,2,1,0:T(8,128)(2,1)} %p_hbm.1), custom_call_target="tpu_custom_call" | custom-call | tf_op jit(solution)/shard_map/edges/pallas_call | solution.py:389
  32.9 2.0 %collective-permute-start.2 = (bf16[64,64,128]{2,1,0:T(8,128)(2,1)S(1)}, bf16[64,64,128]{2,1,0:T(8,128)(2,1)S(1)}, u32[]{:S(2)}, u32[]{:S(2)}) collective-permute-start(bf16[64,64,128]{2,1,0:T(8,128)(2,1)S(1)} %get-tuple-element.26), channel_id=1, source_target_pairs={{0,8},{8,0},{16,24},{24,16},{32,40},{40,32},{48,56},{56,48},{64,72... | collective-permute-start | bytes 3145736 | tf_op jit(solution)/shard_map/ppermute | solution.py:398
  34.9 7.1 %collective-permute-start.3 = (bf16[64,64,128]{2,1,0:T(8,128)(2,1)}, bf16[64,64,128]{2,1,0:T(8,128)(2,1)S(1)}, u32[]{:S(2)}, u32[]{:S(2)}) collective-permute-start(bf16[64,64,128]{2,1,0:T(8,128)(2,1)} %get-tuple-element.27), channel_id=1, source_target_pairs={{0,0},{8,16},{16,8},{24,32},{32,24},{40,48},{48,40},{56,64},{64,56... | collective-permute-start | bytes 3145736 | tf_op jit(solution)/shard_map/ppermute | solution.py:399
  42.0 0.0 collective-permute-start
  42.1 2.9 %collective-permute-start.1 = (bf16[4,1,64,128]{3,2,1,0:T(8,128)(2,1)S(1)}, bf16[4,1,64,128]{3,2,1,0:T(8,128)(2,1)S(1)}, u32[]{:S(2)}, u32[]{:S(2)}) collective-permute-start(bf16[4,1,64,128]{3,2,1,0:T(8,128)(2,1)S(1)} %get-tuple-element.21), channel_id=1, source_target_pairs={{0,7},{1,0},{2,1},{3,2},{4,3},{5,4},{6,5},{7,6},{8,15},{9,8},{10,9... | collective-permute-start | bytes 196616 | tf_op jit(solution)/shard_map/ppermute | solution.py:379
  45.7 0.7 broadcast_add_fusion
  46.3 1.3 %fusion.13 = (s32[1024]{0:T(1024)}, s32[1024]{0:T(1024)}, s32[1024]{0:T(1024)}) fusion(s32[1024]{0:T(1024)} %bitcast.9, s32[1024]{0:T(1024)S(1)} %bitcast.8, s32[]{:T(128)} %bitcast.6, s32[1024]{0:T(1024)} %bitcast.10, pred[]{:T(512)S(6)} %eq.30, pred[]{:T(512)S(6)} %eq.26), kind=kLoop, calls=%fused_computation.31 | loop fusion | flops 113664 | bytes 24582 | tf_op jit(solution)/shard_map/jit(_where)/select_n | solution.py:368
  47.7 17.2 %galerkin_main.1 = (f32[144,128,896]{2,1,0:T(8,128)}, bf16[32,256,4096]{2,1,0:T(8,128)(2,1)}) custom-call(s32[1,1]{1,0:T(1,128)} %copy.7.live_ref, s32[1024]{0:T(1024)} %get-tuple-element.33.ci_ref, s32[1024]{0:T(1024)} %get-tuple-element.32.zi_ref, s32[1024]{0:T(1024)} %get-tuple-element.31.hp_ref, bf16[64,65536]{1,0:T(8,128)(2,1)} %bitcast.11, ...), custom_call_target="tpu_custom_call" | custom-call | flops 4000000000 | bytes 20000000 | tf_op jit(solution)/shard_map/galerkin_main/pallas_call | solution.py:408
  64.9 0.0 collective-permute-done.yl_ref
  64.9 0.0 collective-permute-done.1.yr_ref
  64.9 2.7 %galerkin_beside.1 = (f32[128,1152]{1,0:T(8,128)S(1)}, f32[128,640]{1,0:T(8,128)S(1)}, f32[128,640]{1,0:T(8,128)S(1)}, bf16[2,256,4096]{2,1,0:T(8,128)(2,1)S(1)}) custom-call(f32[144,128,896]{2,1,0:T(8,128)} %get-tuple-element.18.sums_hbm, bf16[32,256,4096]{2,1,0:T(8,128)(2,1)} %get-tuple-element.19.wt_hbm, ...), custom_call_target="tpu_custom_call" | custom-call | flops 200000000 | bytes 10000000 | tf_op jit(solution)/shard_map/galerkin_beside/pallas_call | solution.py:436
  67.6 0.0 collective-permute-done.2.ha_ref
  67.7 0.0 collective-permute-done.3.hb_ref
  67.7 1.4 %galerkin_halo.1 = (f32[128,1152]{1,0:T(8,128)S(1)}, bf16[128,640]{1,0:T(8,128)(2,1)S(1)}, bf16[128,640]{1,0:T(8,128)(2,1)S(1)}) custom-call(f32[128,1152]{1,0:T(8,128)S(1)} %get-tuple-element.22.own_in, f32[128,640]{1,0:T(8,128)S(1)} %get-tuple-element.23.up_in, f32[128,640]{1,0:T(8,128)S(1)} %get-tuple-element.24.dn_in, ...), custom_call_target="tpu_custom_call" | custom-call | flops 600000000 | bytes 8000000 | tf_op jit(solution)/shard_map/galerkin_halo/pallas_call | solution.py:458
  69.1 0.1 collective-permute-start.4
  69.2 3.4 %collective-permute-start.5 = (bf16[128,640]{1,0:T(8,128)(2,1)S(1)}, bf16[128,640]{1,0:T(8,128)(2,1)S(1)}, u32[]{:S(2)}, u32[]{:S(2)}) collective-permute-start(bf16[128,640]{1,0:T(8,128)(2,1)S(1)} %get-tuple-element.30), channel_id=1, source_target_pairs={{0,0},{8,16},{16,8},{24,32},{32,24},{40,48},{48,40},{56,64},{64,56... | collective-permute-start | bytes 491528 | tf_op jit(solution)/shard_map/ppermute | solution.py:469
  72.6 1.9 %collective-permute-done.4.ra_ref = bf16[128,640]{1,0:T(8,128)(2,1)S(1)} collective-permute-done((bf16[128,640]{1,0:T(8,128)(2,1)S(1)}, bf16[128,640]{1,0:T(8,128)(2,1)S(1)}, u32[]{:S(2)}, u32[]{:S(2)}) %collective-permute-start.4) | collective-permute-done | bytes 163872 | tf_op jit(solution)/shard_map/ppermute | solution.py:468
  74.5 4.0 %collective-permute-done.5.rb_ref = bf16[128,640]{1,0:T(8,128)(2,1)S(1)} collective-permute-done((bf16[128,640]{1,0:T(8,128)(2,1)S(1)}, bf16[128,640]{1,0:T(8,128)(2,1)S(1)}, u32[]{:S(2)}, u32[]{:S(2)}) %collective-permute-start.5) | collective-permute-done | bytes 163872 | tf_op jit(solution)/shard_map/ppermute | solution.py:469
  78.5 0.9 %galerkin_sum.1 = f32[128,1152]{1,0:T(8,128)} custom-call(f32[128,1152]{1,0:T(8,128)S(1)} %get-tuple-element.28.own_ref, bf16[128,640]{1,0:T(8,128)(2,1)S(1)} %collective-permute-done.4.ra_ref, bf16[128,640]{1,0:T(8,128)(2,1)S(1)} %collective-permute-done.5.rb_ref), custom_call_target="tpu_custom_call" | custom-call | tf_op jit(solution)/shard_map/galerkin_sum/pallas_call | solution.py:471
Async XLA Ops:
  32.9 34.7 %collective-permute-start.2 = (bf16[64,64,128]{2,1,0:T(8,128)(2,1)S(1)}, bf16[64,64,128]{2,1,0:T(8,128)(2,1)S(1)}, u32[]{:S(2)}, u32[]{:S(2)}) collective-permute-start(bf16[64,64,128]{2,1,0:T(8,128)(2,1)S(1)} %get-tuple-element.26), channel_id=1, source_target_pairs={{0,8},{8,0},{16,24},{24,16},{32,40},{40,32},{48,56},{56,48},{64,72... | collective-permute-start | bytes 3145736 | tf_op jit(solution)/shard_map/ppermute | solution.py:398
  34.9 32.7 %collective-permute-start.3 = (bf16[64,64,128]{2,1,0:T(8,128)(2,1)}, bf16[64,64,128]{2,1,0:T(8,128)(2,1)S(1)}, u32[]{:S(2)}, u32[]{:S(2)}) collective-permute-start(bf16[64,64,128]{2,1,0:T(8,128)(2,1)} %get-tuple-element.27), channel_id=1, source_target_pairs={{0,0},{8,16},{16,8},{24,32},{32,24},{40,48},{48,40},{56,64},{64,56... | collective-permute-start | bytes 3145736 | tf_op jit(solution)/shard_map/ppermute | solution.py:399
  42.0 22.9 %collective-permute-start = (bf16[4,1,64,128]{3,2,1,0:T(8,128)(2,1)S(1)}, bf16[4,1,64,128]{3,2,1,0:T(8,128)(2,1)S(1)}, u32[]{:S(2)}, u32[]{:S(2)}) collective-permute-start(bf16[4,1,64,128]{3,2,1,0:T(8,128)(2,1)S(1)} %get-tuple-element.20), channel_id=1, source_target_pairs={{0,1},{1,2},{2,3},{3,4},{4,5},{5,6},{6,7},{7,0},{8,9},{9,10},{10,1... | collective-permute-start | bytes 196616 | tf_op jit(solution)/shard_map/ppermute | solution.py:379
  42.1 22.9 %collective-permute-start.1 = (bf16[4,1,64,128]{3,2,1,0:T(8,128)(2,1)S(1)}, bf16[4,1,64,128]{3,2,1,0:T(8,128)(2,1)S(1)}, u32[]{:S(2)}, u32[]{:S(2)}) collective-permute-start(bf16[4,1,64,128]{3,2,1,0:T(8,128)(2,1)S(1)} %get-tuple-element.21), channel_id=1, source_target_pairs={{0,7},{1,0},{2,1},{3,2},{4,3},{5,4},{6,5},{7,6},{8,15},{9,8},{10,9... | collective-permute-start | bytes 196616 | tf_op jit(solution)/shard_map/ppermute | solution.py:379
  69.1 5.4 %collective-permute-start.4 = (bf16[128,640]{1,0:T(8,128)(2,1)S(1)}, bf16[128,640]{1,0:T(8,128)(2,1)S(1)}, u32[]{:S(2)}, u32[]{:S(2)}) collective-permute-start(bf16[128,640]{1,0:T(8,128)(2,1)S(1)} %get-tuple-element.29), channel_id=1, source_target_pairs={{0,8},{8,0},{16,24},{24,16},{32,40},{40,32},{48,56},{56,48},{64,72... | collective-permute-start | bytes 491528 | tf_op jit(solution)/shard_map/ppermute | solution.py:468
  69.2 9.3 %collective-permute-start.5 = (bf16[128,640]{1,0:T(8,128)(2,1)S(1)}, bf16[128,640]{1,0:T(8,128)(2,1)S(1)}, u32[]{:S(2)}, u32[]{:S(2)}) collective-permute-start(bf16[128,640]{1,0:T(8,128)(2,1)S(1)} %get-tuple-element.30), channel_id=1, source_target_pairs={{0,0},{8,16},{16,8},{24,32},{32,24},{40,48},{48,40},{56,64},{64,56... | collective-permute-start | bytes 491528 | tf_op jit(solution)/shard_map/ppermute | solution.py:469

commit v3 on v2

--- a/solution.py
+++ b/solution.py
@@ -389,7 +389,7 @@
     x_a, x_b, p_right, p_left = pl.pallas_call(
         edges_kernel,
         in_specs=[hbm],
-        out_specs=[hbm] * 4,
+        out_specs=[vmem] * 4,
         out_shape=[row, row, column, column],
         scratch_shapes=[pltpu.SemaphoreType.DMA((4,))],
         compiler_params=pltpu.CompilerParams(vmem_limit_bytes=52 * MIB),

time: 81.1 us -> 49.8 us (0.61)
  the two profiles are of different devices: /device:TPU:6 before, /device:TPU:2 now
where the time goes in v3:
time: 49.8 us; the launch traced here: 48.8 us
  Pallas kernels  24.8 us (50%)
  starting transfers between devices  15.7 us (32%)
  waiting for transfers between devices  5.48 us (11%)
  other arithmetic  2.02 us (4%)
  between operations  0.74 us (1%)
    pallas_call x1, Pallas kernels, on_device(): pl.pallas_call(main_kernel, in_specs=[smem, smem, smem, smem, hbm, hbm],...  17.3 us
    ppermute x1, starting transfers between devices, on_device(): halo_b = lax.ppermute(x_b, 'row', pairs_b)  6.81 us
    ppermute x1, waiting for transfers between devices, on_device(): from_b = lax.ppermute(to_b, 'row', pairs_b)  4.02 us
    ppermute x1, starting transfers between devices, on_device(): from_b = lax.ppermute(to_b, 'row', pairs_b)  3.85 us
    ppermute x2, starting transfers between devices, ring(): return lax.ppermute(x, axis, [(k, (k + step) % n) for k in range(n)])  2.96 us
    pallas_call x1, Pallas kernels, on_device(): pl.pallas_call(beside_kernel, in_specs=[hbm] * 2 + [vmem] * 2, out_specs=...  2.69 us
    pallas_call x1, Pallas kernels, on_device(): pl.pallas_call(edges_kernel, in_specs=[hbm], out_specs=[vmem] * 4, out_sh...  2.54 us
    ppermute x1, starting transfers between devices, on_device(): halo_a = lax.ppermute(x_a, 'row', pairs_a)  2 us
  transfers between devices with their start and end apart: 6, of which 2 were waited for; matrix products, arithmetic and copies ran while one was open for 4% of the time, Pallas kernels for 41%

profile of v3, /device:TPU:2, one launch (start us, length us, event | category | flops | bytes accessed | tf_op | source)
XLA Modules:
  0.0 48.8 jit_solution(10867588186194423271)
XLA Ops:
  0.0 2.5 %edges.1 = (bf16[64,64,128]{2,1,0:T(8,128)(2,1)S(1)}, bf16[64,64,128]{2,1,0:T(8,128)(2,1)}, bf16[4,1,64,128]{3,2,1,0:T(8,128)(2,1)S(1)}, bf16[4,1,64,128]{3,2,1,0:T(8,128)(2,1)S(1)}) custom-call(bf16[4,64,64,128]{3,2,1,0:T(8,128)(2,1)} %p_hbm.1), custom_call_target="tpu_custom_call" | custom-call | tf_op jit(solution)/shard_map/edges/pallas_call | solution.py:389
  2.6 2.0 %collective-permute-start.2 = (bf16[64,64,128]{2,1,0:T(8,128)(2,1)S(1)}, bf16[64,64,128]{2,1,0:T(8,128)(2,1)S(1)}, u32[]{:S(2)}, u32[]{:S(2)}) collective-permute-start(bf16[64,64,128]{2,1,0:T(8,128)(2,1)S(1)} %get-tuple-element.26), channel_id=1, source_target_pairs={{0,8},{8,0},{16,24},{24,16},{32,40},{40,32},{48,56},{56,48},{64,72... | collective-permute-start | bytes 3145736 | tf_op jit(solution)/shard_map/ppermute | solution.py:398
  4.6 6.8 %collective-permute-start.3 = (bf16[64,64,128]{2,1,0:T(8,128)(2,1)}, bf16[64,64,128]{2,1,0:T(8,128)(2,1)S(1)}, u32[]{:S(2)}, u32[]{:S(2)}) collective-permute-start(bf16[64,64,128]{2,1,0:T(8,128)(2,1)} %get-tuple-element.27), channel_id=1, source_target_pairs={{0,0},{8,16},{16,8},{24,32},{32,24},{40,48},{48,40},{56,64},{64,56... | collective-permute-start | bytes 3145736 | tf_op jit(solution)/shard_map/ppermute | solution.py:399
  11.4 0.0 collective-permute-start
  11.4 2.9 %collective-permute-start.1 = (bf16[4,1,64,128]{3,2,1,0:T(8,128)(2,1)S(1)}, bf16[4,1,64,128]{3,2,1,0:T(8,128)(2,1)S(1)}, u32[]{:S(2)}, u32[]{:S(2)}) collective-permute-start(bf16[4,1,64,128]{3,2,1,0:T(8,128)(2,1)S(1)} %get-tuple-element.21), channel_id=1, source_target_pairs={{0,7},{1,0},{2,1},{3,2},{4,3},{5,4},{6,5},{7,6},{8,15},{9,8},{10,9... | collective-permute-start | bytes 196616 | tf_op jit(solution)/shard_map/ppermute | solution.py:379
  15.0 0.7 %broadcast_add_fusion = s32[1,1,1024]{2,1,0:T(1,128)S(1)} fusion(s32[1,1,1024]{2,1,0:T(1,128)} %param.9), kind=kLoop, calls=%fused_computation.54 | loop fusion | flops 1024 | bytes 8192 | tf_op jit(solution)/shard_map/sub | solution.py:355
  15.7 1.3 %fusion.13 = (s32[1024]{0:T(1024)}, s32[1024]{0:T(1024)}, s32[1024]{0:T(1024)}) fusion(s32[1024]{0:T(1024)} %bitcast.9, s32[1024]{0:T(1024)S(1)} %bitcast.8, s32[]{:T(128)} %bitcast.6, s32[1024]{0:T(1024)} %bitcast.10, pred[]{:T(512)S(6)} %eq.30, pred[]{:T(512)S(6)} %eq.26), kind=kLoop, calls=%fused_computation.31 | loop fusion | flops 113664 | bytes 24582 | tf_op jit(solution)/shard_map/jit(_where)/select_n | solution.py:368
  17.0 17.3 %galerkin_main.1 = (f32[144,128,896]{2,1,0:T(8,128)}, bf16[32,256,4096]{2,1,0:T(8,128)(2,1)}) custom-call(s32[1,1]{1,0:T(1,128)} %copy.7.live_ref, s32[1024]{0:T(1024)} %get-tuple-element.33.ci_ref, s32[1024]{0:T(1024)} %get-tuple-element.32.zi_ref, s32[1024]{0:T(1024)} %get-tuple-element.31.hp_ref, bf16[64,65536]{1,0:T(8,128)(2,1)} %bitcast.11, ...), custom_call_target="tpu_custom_call" | custom-call | flops 4000000000 | bytes 20000000 | tf_op jit(solution)/shard_map/galerkin_main/pallas_call | solution.py:408
  34.3 0.0 collective-permute-done.yl_ref
  34.3 0.0 collective-permute-done.1.yr_ref
  34.3 2.7 %galerkin_beside.1 = (f32[128,1152]{1,0:T(8,128)S(1)}, f32[128,640]{1,0:T(8,128)S(1)}, f32[128,640]{1,0:T(8,128)S(1)}, bf16[2,256,4096]{2,1,0:T(8,128)(2,1)S(1)}) custom-call(f32[144,128,896]{2,1,0:T(8,128)} %get-tuple-element.18.sums_hbm, bf16[32,256,4096]{2,1,0:T(8,128)(2,1)} %get-tuple-element.19.wt_hbm, ...), custom_call_target="tpu_custom_call" | custom-call | flops 200000000 | bytes 10000000 | tf_op jit(solution)/shard_map/galerkin_beside/pallas_call | solution.py:436
  37.0 0.0 collective-permute-done.2.ha_ref
  37.0 0.0 collective-permute-done.3.hb_ref
  37.0 1.4 %galerkin_halo.1 = (f32[128,1152]{1,0:T(8,128)S(1)}, bf16[128,640]{1,0:T(8,128)(2,1)S(1)}, bf16[128,640]{1,0:T(8,128)(2,1)S(1)}) custom-call(f32[128,1152]{1,0:T(8,128)S(1)} %get-tuple-element.22.own_in, f32[128,640]{1,0:T(8,128)S(1)} %get-tuple-element.23.up_in, f32[128,640]{1,0:T(8,128)S(1)} %get-tuple-element.24.dn_in, ...), custom_call_target="tpu_custom_call" | custom-call | flops 600000000 | bytes 8000000 | tf_op jit(solution)/shard_map/galerkin_halo/pallas_call | solution.py:458
  38.4 0.1 collective-permute-start.4
  38.6 3.8 %collective-permute-start.5 = (bf16[128,640]{1,0:T(8,128)(2,1)S(1)}, bf16[128,640]{1,0:T(8,128)(2,1)S(1)}, u32[]{:S(2)}, u32[]{:S(2)}) collective-permute-start(bf16[128,640]{1,0:T(8,128)(2,1)S(1)} %get-tuple-element.30), channel_id=1, source_target_pairs={{0,0},{8,16},{16,8},{24,32},{32,24},{40,48},{48,40},{56,64},{64,56... | collective-permute-start | bytes 491528 | tf_op jit(solution)/shard_map/ppermute | solution.py:469
  42.4 1.5 %collective-permute-done.4.ra_ref = bf16[128,640]{1,0:T(8,128)(2,1)S(1)} collective-permute-done((bf16[128,640]{1,0:T(8,128)(2,1)S(1)}, bf16[128,640]{1,0:T(8,128)(2,1)S(1)}, u32[]{:S(2)}, u32[]{:S(2)}) %collective-permute-start.4) | collective-permute-done | bytes 163872 | tf_op jit(solution)/shard_map/ppermute | solution.py:468
  43.9 4.0 %collective-permute-done.5.rb_ref = bf16[128,640]{1,0:T(8,128)(2,1)S(1)} collective-permute-done((bf16[128,640]{1,0:T(8,128)(2,1)S(1)}, bf16[128,640]{1,0:T(8,128)(2,1)S(1)}, u32[]{:S(2)}, u32[]{:S(2)}) %collective-permute-start.5) | collective-permute-done | bytes 163872 | tf_op jit(solution)/shard_map/ppermute | solution.py:469
  47.9 0.9 %galerkin_sum.1 = f32[128,1152]{1,0:T(8,128)} custom-call(f32[128,1152]{1,0:T(8,128)S(1)} %get-tuple-element.28.own_ref, bf16[128,640]{1,0:T(8,128)(2,1)S(1)} %collective-permute-done.4.ra_ref, bf16[128,640]{1,0:T(8,128)(2,1)S(1)} %collective-permute-done.5.rb_ref), custom_call_target="tpu_custom_call" | custom-call | tf_op jit(solution)/shard_map/galerkin_sum/pallas_call | solution.py:471
Async XLA Ops:
  2.6 34.5 %collective-permute-start.2 = (bf16[64,64,128]{2,1,0:T(8,128)(2,1)S(1)}, bf16[64,64,128]{2,1,0:T(8,128)(2,1)S(1)}, u32[]{:S(2)}, u32[]{:S(2)}) collective-permute-start(bf16[64,64,128]{2,1,0:T(8,128)(2,1)S(1)} %get-tuple-element.26), channel_id=1, source_target_pairs={{0,8},{8,0},{16,24},{24,16},{32,40},{40,32},{48,56},{56,48},{64,72... | collective-permute-start | bytes 3145736 | tf_op jit(solution)/shard_map/ppermute | solution.py:398
  4.6 32.5 %collective-permute-start.3 = (bf16[64,64,128]{2,1,0:T(8,128)(2,1)}, bf16[64,64,128]{2,1,0:T(8,128)(2,1)S(1)}, u32[]{:S(2)}, u32[]{:S(2)}) collective-permute-start(bf16[64,64,128]{2,1,0:T(8,128)(2,1)} %get-tuple-element.27), channel_id=1, source_target_pairs={{0,0},{8,16},{16,8},{24,32},{32,24},{40,48},{48,40},{56,64},{64,56... | collective-permute-start | bytes 3145736 | tf_op jit(solution)/shard_map/ppermute | solution.py:399
  11.4 22.9 %collective-permute-start = (bf16[4,1,64,128]{3,2,1,0:T(8,128)(2,1)S(1)}, bf16[4,1,64,128]{3,2,1,0:T(8,128)(2,1)S(1)}, u32[]{:S(2)}, u32[]{:S(2)}) collective-permute-start(bf16[4,1,64,128]{3,2,1,0:T(8,128)(2,1)S(1)} %get-tuple-element.20), channel_id=1, source_target_pairs={{0,1},{1,2},{2,3},{3,4},{4,5},{5,6},{6,7},{7,0},{8,9},{9,10},{10,1... | collective-permute-start | bytes 196616 | tf_op jit(solution)/shard_map/ppermute | solution.py:379
  11.4 22.9 %collective-permute-start.1 = (bf16[4,1,64,128]{3,2,1,0:T(8,128)(2,1)S(1)}, bf16[4,1,64,128]{3,2,1,0:T(8,128)(2,1)S(1)}, u32[]{:S(2)}, u32[]{:S(2)}) collective-permute-start(bf16[4,1,64,128]{3,2,1,0:T(8,128)(2,1)S(1)} %get-tuple-element.21), channel_id=1, source_target_pairs={{0,7},{1,0},{2,1},{3,2},{4,3},{5,4},{6,5},{7,6},{8,15},{9,8},{10,9... | collective-permute-start | bytes 196616 | tf_op jit(solution)/shard_map/ppermute | solution.py:379
  38.4 5.4 %collective-permute-start.4 = (bf16[128,640]{1,0:T(8,128)(2,1)S(1)}, bf16[128,640]{1,0:T(8,128)(2,1)S(1)}, u32[]{:S(2)}, u32[]{:S(2)}) collective-permute-start(bf16[128,640]{1,0:T(8,128)(2,1)S(1)} %get-tuple-element.29), channel_id=1, source_target_pairs={{0,8},{8,0},{16,24},{24,16},{32,40},{40,32},{48,56},{56,48},{64,72... | collective-permute-start | bytes 491528 | tf_op jit(solution)/shard_map/ppermute | solution.py:468
  38.6 9.3 %collective-permute-start.5 = (bf16[128,640]{1,0:T(8,128)(2,1)S(1)}, bf16[128,640]{1,0:T(8,128)(2,1)S(1)}, u32[]{:S(2)}, u32[]{:S(2)}) collective-permute-start(bf16[128,640]{1,0:T(8,128)(2,1)S(1)} %get-tuple-element.30), channel_id=1, source_target_pairs={{0,0},{8,16},{16,8},{24,32},{32,24},{40,48},{48,40},{56,64},{64,56... | collective-permute-start | bytes 491528 | tf_op jit(solution)/shard_map/ppermute | solution.py:469
